TPU v7x, 256 devices: a whole 4x4x8 slice. The times are simulated.
256 devices in a mesh: band: 16 (over x, y), grow: 4 (over z_hi), gcol: 4 (over z_lo, core).
Axes of the slice: x: 4, y: 4, z: 8 (z_hi: 4, z_lo: 2; z = z_hi * 2 + z_lo), core: 2. Of those that a mesh axis runs over, the one named last changes fastest.
Arguments:
- valence: bfloat16 [4, 110592], replicated, may hold values from -6 to 6
- conduction: bfloat16 [256, 110592], P(('band', 'grow', 'gcol')), may hold values from -6 to 6
- val_energy: float32 [4], replicated, may hold values from -1 to 0
- cond_energy: float32 [256], replicated, may hold values from 0.2 to 3
- frequencies: float32 [2], replicated, may hold values from 0.1 to 2
- gvec_index: int32 [2048], replicated, may hold values from 0 to 110591, as said below
- first_band: int32 [4], replicated, may hold values from 0 to 127
Outputs:
- chi_zero: bfloat16 [2048, 2, 2, 2048], P(('grow', 'band'), None, None, 'gcol')
Inputs may be any that keep to these rules, and one draw needn't show every extreme that they name: `gvec_index`: all 2048 entries are different.
All inputs are finite; a program needn't handle non-finite values.
Results may differ from a plain program's by a relative error of at most 0.0059.
Values may be sent and summed in bfloat16 or wider, within the bound.
No kernel may reach another device: no remote copies, remote signals or barrier semaphores. Data moves between devices by JAX's collectives and lax.ppermute only.
A program may use at most 128 MiB of HBM per device.

v0:
```python
import numpy as np
import jax
import jax.numpy as jnp
from jax import lax
from jax.experimental import pallas as pl
from jax.experimental.pallas import tpu as pltpu
from jax.sharding import Mesh, PartitionSpec as P
import ml_dtypes

GRID = 48
HALF = GRID // 2 + 1
BF = jnp.bfloat16
ZED = ("grow", "zlo", "core")


def split_table(table):
    high = table.astype(ml_dtypes.bfloat16)
    low = (table - high.astype(np.float64)).astype(ml_dtypes.bfloat16)
    return high, low


def wave(left, right):
    angle = 2.0 * np.pi * (np.outer(left, right) % GRID) / GRID
    return np.cos(angle), np.sin(angle)


def tables():
    line = np.arange(GRID)
    cos, sin = wave(np.arange(HALF), line)
    first = np.zeros((2, HALF, 2, 4, 256))
    for odd in range(2):
        for b in range(4):
            at = 64 * odd + GRID * b
            first[odd, :, 0, b, at : at + GRID] = cos
            first[odd, :, 1, b, at : at + GRID] = -sin
    first = first.reshape(2, HALF * 8, 256)
    cos, sin = wave(line, line)
    order = np.zeros((2, GRID, 12, 2, 4))
    byb = cos.reshape(GRID, 12, 4)
    bys = sin.reshape(GRID, 12, 4)
    order[0, :, :, 0], order[0, :, :, 1] = byb, bys
    order[1, :, :, 0], order[1, :, :, 1] = -bys, byb
    second = order.reshape(2 * GRID, 2 * GRID)
    third = np.zeros((2, 2, GRID, 2, 128))
    for v in range(2):
        at = slice(GRID * v, GRID * v + GRID)
        third[v, 0, :, 0, at], third[v, 0, :, 1, at] = cos, sin
        third[v, 1, :, 0, at], third[v, 1, :, 1, at] = -sin, cos
    third = third.reshape(4 * GRID, 256)
    fh, fl = split_table(first)
    first = np.concatenate([fh, fl], 1)
    sh, sl = split_table(second)
    second = np.concatenate(
        [np.concatenate([sh, sh], 1), np.concatenate([sl, np.zeros_like(sl)], 1)], 0
    )
    th, tl = split_table(third)
    third = np.concatenate([th, tl], 0)
    return first, second, third


def dot_nt(a, b):
    return lax.dot_general(a, b, (((1,), (1,)), ((), ())), preferred_element_type=jnp.float32)


def dot_nn(a, b):
    return jnp.dot(a, b, preferred_element_type=jnp.float32)


def split(value):
    high = value.astype(BF)
    return high, (value - high.astype(jnp.float32)).astype(BF)


def density_kernel(cond, val, gvec, first, second, third, out, xh, xl, u, yh, yl, z, dens):
    zero = jnp.zeros((32, xh.shape[1]), BF)
    con = cond[...].astype(jnp.float32)
    for v in range(4):
        at = 128 * (v // 2) + GRID * (v % 2)
        high, low = split(con * val[v].astype(jnp.float32))
        xh[at : at + GRID, :] = high
        xl[at : at + GRID, :] = low
    for p in range(2):
        xh[128 * p + 96 : 128 * p + 128, :] = zero
        xl[128 * p + 96 : 128 * p + 128, :] = zero
    n1 = HALF * 8
    for pair in range(6):
        both = []
        for odd in range(2):
            start = 384 * pair + 128 * odd
            one = dot_nt(first[odd], xh[:, start : start + 256])
            two = dot_nt(first[odd, :n1], xl[:, start : start + 256])
            both.append((one[:n1] + one[n1:] + two).reshape(HALF, 8, 256))
        high, low = split(jnp.concatenate(both, 1))
        u[:, 16 * pair : 16 * pair + 16, :] = high
        u[:, 96 + 16 * pair : 96 + 16 * pair + 16, :] = low
    for k in range(HALF):
        full = dot_nn(second[...], u[k])
        high, low = split(full[:96] + full[96:])
        for p in range(2):
            for s in range(2):
                rows, lanes = slice(GRID * s, GRID * s + GRID), slice(128 * p, 128 * p + 128)
                put = (p, slice(GRID * k, GRID * k + GRID), slice(128 * s, 128 * s + 128))
                yh[put] = high[rows, lanes]
                yl[put] = low[rows, lanes]
    fill = yh.shape[1] - GRID * HALF
    blank = jnp.zeros((fill, 256), BF)
    for p in range(2):
        yh[p, GRID * HALF :, :] = blank
        yl[p, GRID * HALF :, :] = blank
        one = dot_nt(third[...], yh[p])
        two = dot_nt(third[:192], yl[p])
        z[192 * p : 192 * p + 192, :] = ((one[:192] + one[192:] + two) * GRID ** (-1.5)).astype(BF)
    for c in range(8):
        lanes = slice(256 * c, 256 * c + 256)
        g = gvec[:, lanes]
        plane = lax.shift_right_logical(lax.shift_right_logical(g, 4) * 43691, 17)
        k3 = g - plane * GRID
        k1 = lax.shift_right_logical(lax.shift_right_logical(plane, 4) * 43691, 17)
        k2 = plane - k1 * GRID
        flip = k3 >= HALF
        k1 = jnp.where(flip & (k1 > 0), GRID - k1, k1)
        k2 = jnp.where(flip & (k2 > 0), GRID - k2, k2)
        k3 = jnp.where(flip, GRID - k3, k3)
        spot = k3 * GRID + k2
        row = lax.broadcasted_iota(jnp.int32, (z.shape[1], 256), 0)
        hot = jnp.where(row == spot, 1.0, 0.0).astype(BF)
        t = dot_nn(z[...], hot)
        mask = lax.broadcasted_iota(jnp.int32, (GRID, 256), 0) == k1
        sign = jnp.where(flip, -1.0, 1.0)
        lines = []
        for s in range(2):
            for v in range(4):
                at = (2 * v + s) * GRID
                line = jnp.sum(jnp.where(mask, t[at : at + GRID], 0.0), 0, keepdims=True)
                lines.append(line * sign if s else line)
        dens[:, lanes] = jnp.concatenate(lines, 0)
    for i in range(4):
        for j in range(4):
            at = 16 * (4 * i + j)
            both = jnp.concatenate([dens[:, 512 * j : 512 * j + 512], dens[:, 512 * i : 512 * i + 512]], 0)
            out[at : at + 16, :] = both.astype(BF)


def density_call(valence, conduction, gvec_index):
    first, second, third = (jnp.asarray(t) for t in tables())
    cond = conduction.reshape(GRID, GRID * GRID)
    val = valence.reshape(4, GRID, GRID * GRID)
    gvec = gvec_index.reshape(1, -1)
    return pl.pallas_call(
        density_kernel,
        out_shape=jax.ShapeDtypeStruct((256, 512), BF),
        in_specs=[pl.BlockSpec(memory_space=pltpu.VMEM)] * 6,
        out_specs=pl.BlockSpec(memory_space=pltpu.VMEM),
        scratch_shapes=[
            pltpu.VMEM((256, 2304), BF),
            pltpu.VMEM((256, 2304), BF),
            pltpu.VMEM((HALF, 192, 256), BF),
            pltpu.VMEM((2, 1280, 256), BF),
            pltpu.VMEM((2, 1280, 256), BF),
            pltpu.VMEM((384, 1280), BF),
            pltpu.VMEM((8, 2048), jnp.float32),
        ],
        compiler_params=pltpu.CompilerParams(vmem_limit_bytes=48 * 1024 * 1024),
        cost_estimate=pl.CostEstimate(flops=5 * 10**9, bytes_accessed=3 * 10**6, transcendentals=0),
        name="density",
    )(cond, val, gvec, first, second, third)


def shift(array, axis, step):
    size = lax.axis_size(axis)
    return lax.ppermute(array, axis, [(k, (k + step) % size) for k in range(size)])


def weights(bands, val_energy, cond_energy, frequencies, first_band):
    energies = jnp.take(cond_energy, bands)
    gap = energies[:, None] - val_energy[None, :]
    counted = bands[:, None] >= first_band[None, :]
    total = cond_energy.shape[0] * val_energy.shape[0]
    ratio = -4.0 * gap[None] / (gap[None] ** 2 + frequencies[:, None, None] ** 2)
    return jnp.where(counted[None], ratio, 0.0) / total


def on_device(valence, conduction, val_energy, cond_energy, frequencies, gvec_index, first_band):
    sent = density_call(valence, conduction, gvec_index)
    num_gvec = gvec_index.shape[0]
    num_val = valence.shape[0]
    lines = 2 * num_val
    rows_n = lax.axis_size("grow")
    cols_n = lax.axis_size("zlo") * lax.axis_size("core")
    across = lax.axis_size("bx")
    along = lax.axis_size("by")
    group = rows_n * cols_n
    col_tile = num_gvec // cols_n
    row_tile = num_gvec // rows_n
    row_part = row_tile // across
    sent = sent.reshape(group, 2 * lines, col_tile)
    got = lax.all_to_all(sent, ZED, split_axis=0, concat_axis=0, tiled=True)
    cols = got[:, :lines].reshape(group * lines, col_tile)
    rows = got[:, lines:].reshape(group * lines, row_tile)
    x_here = lax.axis_index("bx")
    y_here = lax.axis_index("by")
    parts = []
    for step in range(across):
        target = lax.rem(x_here + step, across)
        part = lax.dynamic_slice_in_dim(rows, target * row_part, row_part, 1)
        block = jnp.concatenate([cols, part], 1)
        parts.append(block if step == 0 else shift(block, "bx", step))
    whole = jnp.stack(parts)
    source = lax.rem(x_here - jnp.arange(across, dtype=jnp.int32) + across, across)
    bands = ((source * along + y_here) * group)[:, None] + jnp.arange(group, dtype=jnp.int32)
    weight = weights(bands.reshape(-1), val_energy, cond_energy, frequencies, first_band)
    right = whole[..., :col_tile].reshape(across * group * lines, col_tile)
    mine = whole[..., col_tile:].reshape(across * group, 2, num_val, row_part)
    left = (weight[:, :, None, :, None] * mine.astype(jnp.float32)[None]).astype(jnp.bfloat16)
    other = jnp.stack([left[:, :, 1], -left[:, :, 0]], 2)
    both = jnp.stack([left, other], 1)
    num_freq = frequencies.shape[0]
    both = both.reshape(num_freq, 2, across * group * lines, along, row_part // along)
    partial = jnp.einsum("wokyr,kh->yrwoh", both, right, preferred_element_type=jnp.float32)
    total = lax.dynamic_index_in_dim(partial, y_here, 0, keepdims=False)
    for step in range(1, along):
        target = lax.rem(y_here + step, along)
        piece = lax.dynamic_index_in_dim(partial, target, 0, keepdims=False)
        total = total + shift(piece.astype(jnp.bfloat16), "by", step).astype(jnp.float32)
    return total.astype(jnp.bfloat16)


def solution(mesh):
    fine = Mesh(mesh.devices.reshape(4, 4, 4, 2, 2), ("bx", "by", "grow", "zlo", "core"))
    return jax.shard_map(
        on_device,
        mesh=fine,
        in_specs=(P(), P(("bx", "by", "grow", "zlo", "core"), None), P(), P(), P(), P(), P()),
        out_specs=P(("grow", "bx", "by"), None, None, ("zlo", "core")),
        check_vma=False,
    )
```

profile of v0, /device:TPU:6, one launch (start us, length us, event | category | flops | bytes accessed | tf_op | source)
XLA Modules:
  0.0 57.8 jit_solution(733407880947867050)
XLA Ops:
  0.0 2.3 %reduce = bf16[110592]{0:T(1024)(128)(2,1)S(1)} reduce(bf16[1,110592]{1,0:T(2,128)(2,1)} %param.11, bf16[]{:T(256)} %constant.85), dimensions={0}, to_apply=%param.11.reduce_sub_computation | reduce | bytes 442370 | tf_op args[1]
  2.3 0.3 reshape.214.cond
  2.8 0.6 copy-done.1
  3.3 0.3 copy-done.2
  3.7 5.8 %density.1 = bf16[256,512]{1,0:T(8,128)(2,1)} custom-call(bf16[48,2304]{1,0:T(8,128)(2,1)S(1)} %reshape.214.cond, bf16[4,48,2304]{2,1,0:T(8,128)(2,1)S(1)} %bitcast.58, s32[1,2048]{1,0:T(1,128)S(1)} %bitcast.59, bf16[2,400,256]{2,1,0:T(8,128)(2,1)S(1)} %copy-done.2, bf16[192,192]{1,0:T(8,128)(2,1)S(1)} %copy-done.4, bf16[384,256]{1,0:T(8,128)(2,1)S(1)} %copy-done.3), custom_call_target="tpu_custom_call" | custom-call | flops 5000000000 | bytes 3000000 | tf_op jit(solution)/shard_map/density/pallas_call | solution.py:149
  9.6 8.6 %all-to-all-start = ((bf16[16,16,512]{2,1,0:T(8,128)(2,1)}), bf16[16,16,512]{2,1,0:T(8,128)(2,1)S(1)}, u32[]{:S(2)}, u32[]{:S(2)}) async-start(bf16[16,16,512]{2,1,0:T(8,128)(2,1)} %bitcast.1), calls=%async_computation | async-start | bytes 524288 | tf_op jit(solution)/shard_map/all_to_all | solution.py:197
  18.4 0.8 %gather_fusion = f32[64]{0:T(128)S(1)} fusion(f32[256]{0:T(256)S(1)} %copy-done, s32[1024]{0:T(1024)S(1)} %pad_clamp_fusion), kind=kCustom, calls=%fused_computation | custom fusion | bytes 768 | tf_op jit(solution)/shard_map/jit(_take)/gather | solution.py:175
  19.3 0.6 %copy-done.9 = f32[2]{0:T(128)S(1)} copy-done((f32[2]{0:T(128)S(1)}, f32[2]{0:T(128)}, u32[]{:S(2)}) %copy-start.9) | copy-done | bytes 32
  19.9 0.6 %copy-done.7 = f32[4]{0:T(128)S(1)} copy-done((f32[4]{0:T(128)S(1)}, f32[4]{0:T(128)}, u32[]{:S(2)}) %copy-start.7) | copy-done | bytes 40
  20.8 0.7 %copy-done.8 = s32[4]{0:T(128)S(1)} copy-done((s32[4]{0:T(128)S(1)}, s32[4]{0:T(128)}, u32[]{:S(2)}) %copy-start.8) | copy-done | bytes 40
  21.6 7.8 %all-to-all-done = bf16[16,16,512]{2,1,0:T(8,128)(2,1)S(1)} async-done(((bf16[16,16,512]{2,1,0:T(8,128)(2,1)}), bf16[16,16,512]{2,1,0:T(8,128)(2,1)S(1)}, u32[]{:S(2)}, u32[]{:S(2)}) %all-to-all-start) | async-done | bytes 262176 | tf_op jit(solution)/shard_map/all_to_all | solution.py:197
  29.4 0.6 collective-permute-start
  30.0 2.4 %collective-permute-start.1 = (bf16[128,640]{1,0:T(8,128)(2,1)S(1)}, bf16[128,640]{1,0:T(8,128)(2,1)S(1)}, u32[]{:S(2)}, u32[]{:S(2)}) collective-permute-start(bf16[128,640]{1,0:T(8,128)(2,1)S(1)} %get-tuple-element.14), channel_id=1, source_target_pairs={{0,128},{64,192},{128,0},{192,64},{1,129},{65,193},{129,1},{193,65... | collective-permute-start | bytes 491528 | tf_op jit(solution)/shard_map/ppermute | solution.py:171
  32.6 0.2 mul.77
  32.8 3.8 %collective-permute-done = bf16[128,640]{1,0:T(8,128)(2,1)S(1)} collective-permute-done((bf16[128,640]{1,0:T(8,128)(2,1)S(1)}, bf16[128,640]{1,0:T(8,128)(2,1)S(1)}, u32[]{:S(2)}, u32[]{:S(2)}) %collective-permute-start) | collective-permute-done | bytes 163872 | tf_op jit(solution)/shard_map/ppermute | solution.py:171
  36.6 2.0 %collective-permute-done.1 = bf16[128,640]{1,0:T(8,128)(2,1)S(1)} collective-permute-done((bf16[128,640]{1,0:T(8,128)(2,1)S(1)}, bf16[128,640]{1,0:T(8,128)(2,1)S(1)}, u32[]{:S(2)}, u32[]{:S(2)}) %collective-permute-start.1) | collective-permute-done | bytes 163872 | tf_op jit(solution)/shard_map/ppermute | solution.py:171
  38.6 3.2 %collective-permute-done.2 = bf16[128,640]{1,0:T(8,128)(2,1)S(1)} collective-permute-done((bf16[128,640]{1,0:T(8,128)(2,1)S(1)}, bf16[128,640]{1,0:T(8,128)(2,1)S(1)}, u32[]{:S(2)}, u32[]{:S(2)}) %collective-permute-start.2) | collective-permute-done | bytes 163872 | tf_op jit(solution)/shard_map/ppermute | solution.py:171
  41.9 0.9 %copy-done.5 = bf16[4,128,640]{2,1,0:T(8,128)(2,1)} copy-done((bf16[4,128,640]{2,1,0:T(8,128)(2,1)}, bf16[4,128,640]{2,1,0:T(8,128)(2,1)S(1)}, u32[]{:S(2)}) %copy-start.5) | copy-done | bytes 655384
  42.8 0.1 copy.25
  42.9 0.2 multiply_convert_fusion
  43.3 0.2 pad_maximum_fusion.1
  43.5 0.4 stack.32
  44.0 0.6 %copy.26 = bf16[2,1,512,4,32]{2,4,3,1,0:T(8,128)(2,1)S(1)} copy(bf16[2,1,512,4,32]{4,3,2,0,1:T(4,128)(2,1)S(1)} %stack.32) | data formatting | bytes 524288 | tf_op jit(solution)/shard_map/stack | solution.py:216
  44.6 1.0 %slice-done = bf16[4,128,512]{2,1,0:T(8,128)(2,1)S(1)} async-done(((bf16[4,128,640]{2,1,0:T(8,128)(2,1)}), bf16[4,128,512]{2,1,0:T(8,128)(2,1)S(1)}, s32[]{:S(2)}) %slice-start) | async-done | bytes 524312 | tf_op jit(solution)/shard_map/slice | solution.py:212
  45.6 0.4 fusion
  46.1 1.6 %collective-permute-start.3 = (bf16[32,2,2,512]{3,0,2,1:T(8,128)(2,1)S(1)}, bf16[32,2,2,512]{3,0,2,1:T(8,128)(2,1)S(1)}, u32[]{:S(2)}, u32[]{:S(2)}) collective-permute-start(bf16[32,2,2,512]{3,0,2,1:T(8,128)(2,1)S(1)} %get-tuple-element.5), channel_id=1, source_target_pairs={{0,16},{16,32},{32,48},{48,0},{1,17},{17,33},{33,49},{49,1},{2,18}... | collective-permute-start | bytes 393224 | tf_op jit(solution)/shard_map/ppermute | solution.py:171
  47.8 1.7 %collective-permute-start.5 = (bf16[32,2,2,512]{3,0,2,1:T(8,128)(2,1)S(1)}, bf16[32,2,2,512]{3,0,2,1:T(8,128)(2,1)S(1)}, u32[]{:S(2)}, u32[]{:S(2)}) collective-permute-start(bf16[32,2,2,512]{3,0,2,1:T(8,128)(2,1)S(1)} %get-tuple-element.6), channel_id=1, source_target_pairs={{0,48},{16,0},{32,16},{48,32},{1,49},{17,1},{33,17},{49,33},{2,50}... | collective-permute-start | bytes 393224 | tf_op jit(solution)/shard_map/ppermute | solution.py:171
  49.4 2.0 %collective-permute-start.4 = (bf16[32,2,2,512]{3,0,2,1:T(8,128)(2,1)S(1)}, bf16[32,2,2,512]{3,0,2,1:T(8,128)(2,1)S(1)}, u32[]{:S(2)}, u32[]{:S(2)}) collective-permute-start(bf16[32,2,2,512]{3,0,2,1:T(8,128)(2,1)S(1)} %get-tuple-element.7), channel_id=1, source_target_pairs={{0,32},{16,48},{32,0},{48,16},{1,33},{17,49},{33,1},{49,17},{2,34}... | collective-permute-start | bytes 393224 | tf_op jit(solution)/shard_map/ppermute | solution.py:171
  51.4 1.5 %collective-permute-done.3 = bf16[32,2,2,512]{3,0,2,1:T(8,128)(2,1)S(1)} collective-permute-done((bf16[32,2,2,512]{3,0,2,1:T(8,128)(2,1)S(1)}, bf16[32,2,2,512]{3,0,2,1:T(8,128)(2,1)S(1)}, u32[]{:S(2)}, u32[]{:S(2)}) %collective-permute-start.3) | collective-permute-done | bytes 131104 | tf_op jit(solution)/shard_map/ppermute | solution.py:171
  52.9 2.2 %collective-permute-done.5 = bf16[32,2,2,512]{3,0,2,1:T(8,128)(2,1)S(1)} collective-permute-done((bf16[32,2,2,512]{3,0,2,1:T(8,128)(2,1)S(1)}, bf16[32,2,2,512]{3,0,2,1:T(8,128)(2,1)S(1)}, u32[]{:S(2)}, u32[]{:S(2)}) %collective-permute-start.5) | collective-permute-done | bytes 131104 | tf_op jit(solution)/shard_map/ppermute | solution.py:171
  55.1 1.8 %collective-permute-done.4 = bf16[32,2,2,512]{3,0,2,1:T(8,128)(2,1)S(1)} collective-permute-done((bf16[32,2,2,512]{3,0,2,1:T(8,128)(2,1)S(1)}, bf16[32,2,2,512]{3,0,2,1:T(8,128)(2,1)S(1)}, u32[]{:S(2)}, u32[]{:S(2)}) %collective-permute-start.4) | collective-permute-done | bytes 131104 | tf_op jit(solution)/shard_map/ppermute | solution.py:171
  57.0 0.8 %copy.30 = bf16[32,2,2,512]{3,2,1,0:T(2,128)(2,1)} copy(bf16[32,2,2,512]{3,0,2,1:T(8,128)(2,1)S(1)} %fusion.6) | data formatting | bytes 262144 | tf_op jit(solution)/shard_map/convert_element_type | solution.py:225
  (41 shorter events, 1.6 us)
Async XLA Ops:
  0.0 18.4 %copy-start = (f32[256]{0:T(256)S(1)}, f32[256]{0:T(256)}, u32[]{:S(2)}) copy-start(f32[256]{0:T(256)} %param.13) | copy-start | bytes 3076
  0.0 2.6 %copy-start.6 = (bf16[4,110592]{1,0:T(4,128)(2,1)S(1)}, bf16[4,110592]{1,0:T(4,128)(2,1)}, u32[]{:S(2)}) copy-start(bf16[4,110592]{1,0:T(4,128)(2,1)} %param.10) | copy-start | bytes 2654212
  2.6 0.7 %copy-start.1 = (s32[2048]{0:T(1024)S(1)}, s32[2048]{0:T(1024)}, u32[]{:S(2)}) copy-start(s32[2048]{0:T(1024)} %param.15) | copy-start | bytes 24580
  2.6 1.0 %copy-start.2 = (bf16[2,400,256]{2,1,0:T(8,128)(2,1)S(1)}, bf16[2,400,256]{2,1,0:T(8,128)(2,1)}, u32[]{:S(2)}) copy-start(bf16[2,400,256]{2,1,0:T(8,128)(2,1)} %constant.81.clone.first) | copy-start | bytes 1228804
  2.6 1.0 %copy-start.3 = (bf16[384,256]{1,0:T(8,128)(2,1)S(1)}, bf16[384,256]{1,0:T(8,128)(2,1)}, u32[]{:S(2)}) copy-start(bf16[384,256]{1,0:T(8,128)(2,1)} %constant.83.clone.third) | copy-start | bytes 589828
  2.6 1.1 %copy-start.4 = (bf16[192,192]{1,0:T(8,128)(2,1)S(1)}, bf16[192,192]{1,0:T(8,128)(2,1)}, u32[]{:S(2)}) copy-start(bf16[192,192]{1,0:T(8,128)(2,1)} %constant.82.clone.second) | copy-start | bytes 221188
  9.6 19.8 %all-to-all-start = ((bf16[16,16,512]{2,1,0:T(8,128)(2,1)}), bf16[16,16,512]{2,1,0:T(8,128)(2,1)S(1)}, u32[]{:S(2)}, u32[]{:S(2)}) async-start(bf16[16,16,512]{2,1,0:T(8,128)(2,1)} %bitcast.1), calls=%async_computation | async-start | bytes 524288 | tf_op jit(solution)/shard_map/all_to_all | solution.py:197
  19.2 0.7 %copy-start.9 = (f32[2]{0:T(128)S(1)}, f32[2]{0:T(128)}, u32[]{:S(2)}) copy-start(f32[2]{0:T(128)} %param.14) | copy-start | bytes 28
  19.9 0.7 %copy-start.7 = (f32[4]{0:T(128)S(1)}, f32[4]{0:T(128)}, u32[]{:S(2)}) copy-start(f32[4]{0:T(128)} %param.12) | copy-start | bytes 52
  20.8 0.7 %copy-start.8 = (s32[4]{0:T(128)S(1)}, s32[4]{0:T(128)}, u32[]{:S(2)}) copy-start(s32[4]{0:T(128)} %param.16) | copy-start | bytes 52
  29.4 7.1 %collective-permute-start = (bf16[128,640]{1,0:T(8,128)(2,1)S(1)}, bf16[128,640]{1,0:T(8,128)(2,1)S(1)}, u32[]{:S(2)}, u32[]{:S(2)}) collective-permute-start(bf16[128,640]{1,0:T(8,128)(2,1)S(1)} %get-tuple-element.13), channel_id=1, source_target_pairs={{0,64},{64,128},{128,192},{192,0},{1,65},{65,129},{129,193},{193,1... | collective-permute-start | bytes 491528 | tf_op jit(solution)/shard_map/ppermute | solution.py:171
  30.0 8.6 %collective-permute-start.1 = (bf16[128,640]{1,0:T(8,128)(2,1)S(1)}, bf16[128,640]{1,0:T(8,128)(2,1)S(1)}, u32[]{:S(2)}, u32[]{:S(2)}) collective-permute-start(bf16[128,640]{1,0:T(8,128)(2,1)S(1)} %get-tuple-element.14), channel_id=1, source_target_pairs={{0,128},{64,192},{128,0},{192,64},{1,129},{65,193},{129,1},{193,65... | collective-permute-start | bytes 491528 | tf_op jit(solution)/shard_map/ppermute | solution.py:171
  32.4 9.4 %collective-permute-start.2 = (bf16[128,640]{1,0:T(8,128)(2,1)S(1)}, bf16[128,640]{1,0:T(8,128)(2,1)S(1)}, u32[]{:S(2)}, u32[]{:S(2)}) collective-permute-start(bf16[128,640]{1,0:T(8,128)(2,1)S(1)} %get-tuple-element.15), channel_id=1, source_target_pairs={{0,192},{64,0},{128,64},{192,128},{1,193},{65,1},{129,65},{193,129... | collective-permute-start | bytes 491528 | tf_op jit(solution)/shard_map/ppermute | solution.py:171
  41.9 0.9 %copy-start.5 = (bf16[4,128,640]{2,1,0:T(8,128)(2,1)}, bf16[4,128,640]{2,1,0:T(8,128)(2,1)S(1)}, u32[]{:S(2)}) copy-start(bf16[4,128,640]{2,1,0:T(8,128)(2,1)S(1)} %pad_maximum_fusion) | copy-start | bytes 1966084
  44.6 1.0 %slice-start = ((bf16[4,128,640]{2,1,0:T(8,128)(2,1)}), bf16[4,128,512]{2,1,0:T(8,128)(2,1)S(1)}, s32[]{:S(2)}) async-start(bf16[4,128,640]{2,1,0:T(8,128)(2,1)} %copy-done.5), calls=%async_computation.1 | async-start | bytes 1048576 | tf_op jit(solution)/shard_map/slice | solution.py:212
  46.1 6.8 %collective-permute-start.3 = (bf16[32,2,2,512]{3,0,2,1:T(8,128)(2,1)S(1)}, bf16[32,2,2,512]{3,0,2,1:T(8,128)(2,1)S(1)}, u32[]{:S(2)}, u32[]{:S(2)}) collective-permute-start(bf16[32,2,2,512]{3,0,2,1:T(8,128)(2,1)S(1)} %get-tuple-element.5), channel_id=1, source_target_pairs={{0,16},{16,32},{32,48},{48,0},{1,17},{17,33},{33,49},{49,1},{2,18}... | collective-permute-start | bytes 393224 | tf_op jit(solution)/shard_map/ppermute | solution.py:171
  47.8 7.3 %collective-permute-start.5 = (bf16[32,2,2,512]{3,0,2,1:T(8,128)(2,1)S(1)}, bf16[32,2,2,512]{3,0,2,1:T(8,128)(2,1)S(1)}, u32[]{:S(2)}, u32[]{:S(2)}) collective-permute-start(bf16[32,2,2,512]{3,0,2,1:T(8,128)(2,1)S(1)} %get-tuple-element.6), channel_id=1, source_target_pairs={{0,48},{16,0},{32,16},{48,32},{1,49},{17,1},{33,17},{49,33},{2,50}... | collective-permute-start | bytes 393224 | tf_op jit(solution)/shard_map/ppermute | solution.py:171
  49.4 7.5 %collective-permute-start.4 = (bf16[32,2,2,512]{3,0,2,1:T(8,128)(2,1)S(1)}, bf16[32,2,2,512]{3,0,2,1:T(8,128)(2,1)S(1)}, u32[]{:S(2)}, u32[]{:S(2)}) collective-permute-start(bf16[32,2,2,512]{3,0,2,1:T(8,128)(2,1)S(1)} %get-tuple-element.7), channel_id=1, source_target_pairs={{0,32},{16,48},{32,0},{48,16},{1,33},{17,49},{33,1},{49,17},{2,34}... | collective-permute-start | bytes 393224 | tf_op jit(solution)/shard_map/ppermute | solution.py:171
where the time goes:
time: 58.8 us; the launch traced here: 57.8 us
  waiting for transfers between devices  22.2 us (38%)
  starting transfers between devices  16.8 us (29%)
  local copies, waits for them, and re-layouts  8.73 us (15%)
  Pallas kernels  5.82 us (10%)
  other arithmetic  3.41 us (6%)
    ppermute x6, waiting for transfers between devices, shift(): lax.ppermute(array, axis, [(k, (k + step) % size) for k in range(size)])  14.5 us
    all_to_all x1, starting transfers between devices, on_device(): got = lax.all_to_all(sent, ZED, split_axis=0, concat_axis=0, tiled=True)  8.57 us
    ppermute x6, starting transfers between devices, shift(): lax.ppermute(array, axis, [(k, (k + step) % size) for k in range(size)])  8.27 us
    all_to_all x1, waiting for transfers between devices, on_device(): got = lax.all_to_all(sent, ZED, split_axis=0, concat_axis=0, tiled=True)  7.75 us
    pallas_call x1, Pallas kernels, density_call(): pl.pallas_call(density_kernel, out_shape=jax.ShapeDtypeStruct((256, 512),...  5.82 us
    unnamed x21, local copies, waits for them, and re-layouts  3.91 us
    unnamed x1, other arithmetic  2.31 us
  transfers between devices with their start and end apart: 7, of which 7 were waited for; matrix products, arithmetic and copies ran while one was open for 3% of the time, Pallas kernels for 0%

commit v1 on v0

--- a/solution.py
+++ b/solution.py
@@ -11,6 +11,7 @@
 HALF = GRID // 2 + 1
 BF = jnp.bfloat16
 ZED = ("grow", "zlo", "core")
+ALL = ("bx", "by") + ZED
 
 
 def split_table(table):
@@ -73,7 +74,7 @@
 
 def density_kernel(cond, val, gvec, first, second, third, out, xh, xl, u, yh, yl, z, dens):
     zero = jnp.zeros((32, xh.shape[1]), BF)
-    con = cond[...].astype(jnp.float32)
+    con = cond[0].astype(jnp.float32)
     for v in range(4):
         at = 128 * (v // 2) + GRID * (v % 2)
         high, low = split(con * val[v].astype(jnp.float32))
@@ -134,16 +135,27 @@
                 line = jnp.sum(jnp.where(mask, t[at : at + GRID], 0.0), 0, keepdims=True)
                 lines.append(line * sign if s else line)
         dens[:, lanes] = jnp.concatenate(lines, 0)
+    quarter = lax.broadcasted_iota(jnp.int32, (8, 128), 1) // 32
     for i in range(4):
+        tiles = [dens[:, 512 * i + 128 * t : 512 * i + 128 * t + 128] for t in range(4)]
+        turned = []
+        for t in range(4):
+            tile = tiles[t]
+            for other in range(4):
+                if other != t:
+                    moved = pltpu.roll(tiles[other], (32 * (other - t)) % 128, 1)
+                    tile = jnp.where(quarter == other, moved, tile)
+            turned.append(tile)
+        orders = (jnp.concatenate(tiles, 1), jnp.concatenate(turned, 1))
         for j in range(4):
             at = 16 * (4 * i + j)
-            both = jnp.concatenate([dens[:, 512 * j : 512 * j + 512], dens[:, 512 * i : 512 * i + 512]], 0)
+            both = jnp.concatenate([dens[:, 512 * j : 512 * j + 512], orders[j % 2]], 0)
             out[at : at + 16, :] = both.astype(BF)
 
 
 def density_call(valence, conduction, gvec_index):
     first, second, third = (jnp.asarray(t) for t in tables())
-    cond = conduction.reshape(GRID, GRID * GRID)
+    cond = jnp.pad(conduction, ((0, 3), (0, 0))).reshape(4, GRID, GRID * GRID)
     val = valence.reshape(4, GRID, GRID * GRID)
     gvec = gvec_index.reshape(1, -1)
     return pl.pallas_call(
@@ -166,71 +178,104 @@
     )(cond, val, gvec, first, second, third)
 
 
-def shift(array, axis, step):
-    size = lax.axis_size(axis)
-    return lax.ppermute(array, axis, [(k, (k + step) % size) for k in range(size)])
-
-
-def weights(bands, val_energy, cond_energy, frequencies, first_band):
-    energies = jnp.take(cond_energy, bands)
-    gap = energies[:, None] - val_energy[None, :]
-    counted = bands[:, None] >= first_band[None, :]
-    total = cond_energy.shape[0] * val_energy.shape[0]
-    ratio = -4.0 * gap[None] / (gap[None] ** 2 + frequencies[:, None, None] ** 2)
-    return jnp.where(counted[None], ratio, 0.0) / total
+def product_kernel(turn, weight, own, one, two, three, mine, first, second, third):
+    cols, lefts = [], []
+    for n, block in enumerate((own, one, two, three)):
+        cols.append(block[:, :512])
+        rows = block[:, 512:640].astype(jnp.float32)
+        rows = pltpu.roll(rows, lax.rem(128 - 32 * turn[0], 128), 1)
+        split_rows = rows.reshape(16, 2, 4, 128)
+        swapped = jnp.concatenate([split_rows[:, 1:], -split_rows[:, :1]], 1).reshape(128, 128)
+        parts = []
+        for freq in range(2):
+            scale = weight[n, :, freq : freq + 1]
+            parts.append((scale * rows).astype(BF))
+            parts.append((scale * swapped).astype(BF))
+        lefts.append(jnp.concatenate(parts, 1))
+    left = jnp.concatenate(lefts, 0)
+    right = jnp.concatenate(cols, 0)
+    total = lax.dot_general(left, right, (((0,), (0,)), ((), ())), preferred_element_type=jnp.float32)
+    for part in range(4):
+        at = 128 * part
+        mine[32 * part : 32 * part + 32, :] = total[at : at + 32]
+        first[32 * part : 32 * part + 32, :] = total[at + 32 : at + 64].astype(BF)
+        second[32 * part : 32 * part + 32, :] = total[at + 64 : at + 96].astype(BF)
+        third[32 * part : 32 * part + 32, :] = total[at + 96 : at + 128].astype(BF)
+
+
+def product_call(turn, weight, blocks):
+    piece = jax.ShapeDtypeStruct((128, 512), BF)
+    vmem = pl.BlockSpec(memory_space=pltpu.VMEM)
+    return pl.pallas_call(
+        product_kernel,
+        out_shape=(jax.ShapeDtypeStruct((128, 512), jnp.float32), piece, piece, piece),
+        in_specs=[pl.BlockSpec(memory_space=pltpu.SMEM)] + [vmem] * 5,
+        out_specs=(vmem,) * 4,
+        compiler_params=pltpu.CompilerParams(vmem_limit_bytes=48 * 1024 * 1024),
+        cost_estimate=pl.CostEstimate(flops=3 * 10**8, bytes_accessed=2 * 10**6, transcendentals=0),
+        name="product",
+    )(turn, weight, *blocks)
+
+
+def ring_pairs(across, along, rest, step, gather):
+    pairs = []
+    for x in range(across):
+        for y in range(along):
+            for z in range(rest):
+                if (z % 2 == 0) == gather:
+                    to = ((x + step) % across, y)
+                else:
+                    to = (x, (y + step) % along)
+                pairs.append(((x * along + y) * rest + z, (to[0] * along + to[1]) * rest + z))
+    return pairs
 
 
 def on_device(valence, conduction, val_energy, cond_energy, frequencies, gvec_index, first_band):
     sent = density_call(valence, conduction, gvec_index)
-    num_gvec = gvec_index.shape[0]
     num_val = valence.shape[0]
     lines = 2 * num_val
-    rows_n = lax.axis_size("grow")
-    cols_n = lax.axis_size("zlo") * lax.axis_size("core")
     across = lax.axis_size("bx")
     along = lax.axis_size("by")
-    group = rows_n * cols_n
-    col_tile = num_gvec // cols_n
-    row_tile = num_gvec // rows_n
-    row_part = row_tile // across
-    sent = sent.reshape(group, 2 * lines, col_tile)
+    group = lax.axis_size("grow") * lax.axis_size("zlo") * lax.axis_size("core")
+    sent = sent.reshape(group, 2 * lines, 512)
     got = lax.all_to_all(sent, ZED, split_axis=0, concat_axis=0, tiled=True)
-    cols = got[:, :lines].reshape(group * lines, col_tile)
-    rows = got[:, lines:].reshape(group * lines, row_tile)
+    cols = got[:, :lines].reshape(group * lines, 512)
+    rows = got[:, lines:].reshape(group * lines, 512)
     x_here = lax.axis_index("bx")
     y_here = lax.axis_index("by")
-    parts = []
-    for step in range(across):
-        target = lax.rem(x_here + step, across)
-        part = lax.dynamic_slice_in_dim(rows, target * row_part, row_part, 1)
+    even = lax.axis_index("core") == 0
+    place = jnp.where(even, x_here, y_here)
+    other = jnp.where(even, y_here, x_here)
+    blocks = {}
+    for step in (0, 1, 3, 2):
+        target = lax.rem(place + step, across)
+        part = lax.dynamic_slice_in_dim(rows, target * 128, 128, 1)
         block = jnp.concatenate([cols, part], 1)
-        parts.append(block if step == 0 else shift(block, "bx", step))
-    whole = jnp.stack(parts)
-    source = lax.rem(x_here - jnp.arange(across, dtype=jnp.int32) + across, across)
-    bands = ((source * along + y_here) * group)[:, None] + jnp.arange(group, dtype=jnp.int32)
-    weight = weights(bands.reshape(-1), val_energy, cond_energy, frequencies, first_band)
-    right = whole[..., :col_tile].reshape(across * group * lines, col_tile)
-    mine = whole[..., col_tile:].reshape(across * group, 2, num_val, row_part)
-    left = (weight[:, :, None, :, None] * mine.astype(jnp.float32)[None]).astype(jnp.bfloat16)
-    other = jnp.stack([left[:, :, 1], -left[:, :, 0]], 2)
-    both = jnp.stack([left, other], 1)
-    num_freq = frequencies.shape[0]
-    both = both.reshape(num_freq, 2, across * group * lines, along, row_part // along)
-    partial = jnp.einsum("wokyr,kh->yrwoh", both, right, preferred_element_type=jnp.float32)
-    total = lax.dynamic_index_in_dim(partial, y_here, 0, keepdims=False)
-    for step in range(1, along):
-        target = lax.rem(y_here + step, along)
-        piece = lax.dynamic_index_in_dim(partial, target, 0, keepdims=False)
-        total = total + shift(piece.astype(jnp.bfloat16), "by", step).astype(jnp.float32)
-    return total.astype(jnp.bfloat16)
+        pairs = ring_pairs(across, along, group, step, True)
+        blocks[step] = lax.ppermute(block, ALL, pairs) if step else block
+    source = lax.rem(place - jnp.arange(across, dtype=jnp.int32) + across, across)
+    band = jnp.where(even, source * along + other, other * along + source)
+    bands = (band * group)[:, None] + jnp.arange(group, dtype=jnp.int32)
+    energies = jnp.take(cond_energy, bands)
+    gap = energies[..., None] - val_energy
+    counted = bands[..., None] >= first_band
+    ratio = -4.0 * gap[..., None] / (gap[..., None] ** 2 + frequencies**2)
+    weight = jnp.where(counted[..., None], ratio, 0.0) / (cond_energy.shape[0] * num_val)
+    weight = jnp.broadcast_to(weight[:, :, None], (across, group, 2, num_val, frequencies.shape[0]))
+    weight = weight.reshape(across, group * lines, frequencies.shape[0])
+    total, *pieces = product_call(other.reshape(1), weight, [blocks[step] for step in range(across)])
+    for step in (1, 3, 2):
+        pairs = ring_pairs(across, along, group, step, False)
+        total = total + lax.ppermute(pieces[step - 1], ALL, pairs).astype(jnp.float32)
+    return jnp.transpose(total.reshape(2, 2, 32, 512), (2, 0, 1, 3)).astype(BF)
 
 
 def solution(mesh):
-    fine = Mesh(mesh.devices.reshape(4, 4, 4, 2, 2), ("bx", "by", "grow", "zlo", "core"))
+    fine = Mesh(mesh.devices.reshape(4, 4, 4, 2, 2), ALL)
     return jax.shard_map(
         on_device,
         mesh=fine,
-        in_specs=(P(), P(("bx", "by", "grow", "zlo", "core"), None), P(), P(), P(), P(), P()),
+        in_specs=(P(), P(ALL, None), P(), P(), P(), P(), P()),
         out_specs=P(("grow", "bx", "by"), None, None, ("zlo", "core")),
         check_vma=False,
     )

time: 58.8 us -> 50.2 us (0.85)
  waiting for transfers between devices: 22.2 us -> 18.6 us
  other arithmetic: 3.41 us -> 0.78 us
  local copies, waits for them, and re-layouts: 8.73 us -> 6.38 us
  Pallas kernels: 5.82 us -> 6.85 us
    ppermute x6, waiting for transfers between devices: 14.5 us -> 10.7 us  [the longest x3 6.25 us: on_device(): blocks[step] = lax.ppermute(block, ALL, pairs) if step else block]
    unnamed x1 -> x0, other arithmetic: 2.31 us -> none
    pad x0 -> x1, local copies, waits for them, and re-layouts: none -> 1.55 us  [density_call(): cond = jnp.pad(conduction, ((0, 3), (0, 0))).reshape(4, GRID, GRID * GRID)]
    unnamed x21 -> x18, local copies, waits for them, and re-layouts: 3.91 us -> 2.82 us
    another operation x2 -> x0, local copies, waits for them, and re-layouts: 1 us -> none  [on_device(): both = jnp.stack([left, other], 1)]
    slice x2 -> x0, local copies, waits for them, and re-layouts: 0.99 us -> none  [on_device(): right = whole[..., :col_tile].reshape(across * group * lines, col_tile)]
    pallas_call x0 -> x1, Pallas kernels: none -> 0.84 us  [product_call(): pl.pallas_call(product_kernel, out_shape=(jax.ShapeDtypeStruct((128, 512)...]
where the time goes in v1:
time: 50.2 us; the launch traced here: 49.6 us
  waiting for transfers between devices  18.6 us (37%)
  starting transfers between devices  16.8 us (33%)
  Pallas kernels  6.85 us (14%)
  local copies, waits for them, and re-layouts  6.38 us (13%)
  other arithmetic  0.78 us (2%)
    all_to_all x1, starting transfers between devices, on_device(): got = lax.all_to_all(sent, ZED, split_axis=0, concat_axis=0, tiled=True)  8.57 us
    all_to_all x1, waiting for transfers between devices, on_device(): got = lax.all_to_all(sent, ZED, split_axis=0, concat_axis=0, tiled=True)  7.9 us
    ppermute x3, waiting for transfers between devices, on_device(): blocks[step] = lax.ppermute(block, ALL, pairs) if step else block  6.25 us
    pallas_call x1, Pallas kernels, density_call(): pl.pallas_call(density_kernel, out_shape=jax.ShapeDtypeStruct((256, 512),...  6.02 us
    ppermute x3, starting transfers between devices, on_device(): lax.ppermute(pieces[step - 1], ALL, pairs).astype(jnp.float32)  5.3 us
    ppermute x3, waiting for transfers between devices, on_device(): lax.ppermute(pieces[step - 1], ALL, pairs).astype(jnp.float32)  4.48 us
    ppermute x3, starting transfers between devices, on_device(): blocks[step] = lax.ppermute(block, ALL, pairs) if step else block  2.97 us
    unnamed x18, local copies, waits for them, and re-layouts  2.82 us
  transfers between devices with their start and end apart: 7, of which 7 were waited for; matrix products, arithmetic and copies ran while one was open for 3% of the time, Pallas kernels for 0%

profile of v1, /device:TPU:6, one launch (start us, length us, event | category | flops | bytes accessed | tf_op | source)
XLA Modules:
  0.0 49.6 jit_solution(10979397603791387032)
XLA Ops:
  0.0 1.5 %pad.4 = bf16[4,110592]{1,0:T(4,128)(2,1)S(1)} pad(bf16[1,110592]{1,0:T(2,128)(2,1)} %param.11, bf16[]{:T(256)} %constant.66.clone.1), padding=0_3x0_0 | pad | bytes 1105922 | tf_op jit(solution)/shard_map/jit(_pad)/pad | solution.py:158
  1.6 0.2 copy_bitcast_fusion
  1.8 0.5 copy-done.1
  2.3 0.3 copy-done.2
  2.7 6.0 %density.1 = bf16[256,512]{1,0:T(8,128)(2,1)} custom-call(bf16[4,48,2304]{2,1,0:T(8,128)(2,1)S(1)} %get-tuple-element.26.cond, bf16[4,48,2304]{2,1,0:T(8,128)(2,1)S(1)} %get-tuple-element.25.val, s32[1,2048]{1,0:T(1,128)S(1)} %bitcast.21, bf16[2,400,256]{2,1,0:T(8,128)(2,1)S(1)} %copy-done.2, bf16[192,192]{1,0:T(8,128)(2,1)S(1)} %copy-done.4, ...), custom_call_target="tpu_custom_call" | custom-call | flops 5000000000 | bytes 3000000 | tf_op jit(solution)/shard_map/density/pallas_call | solution.py:161
  8.7 8.6 %all-to-all-start = ((bf16[16,16,512]{2,1,0:T(8,128)(2,1)}), bf16[16,16,512]{2,1,0:T(8,128)(2,1)S(1)}, u32[]{:S(2)}, u32[]{:S(2)}) async-start(bf16[16,16,512]{2,1,0:T(8,128)(2,1)} %bitcast.3), calls=%async_computation | async-start | bytes 524288 | tf_op jit(solution)/shard_map/all_to_all | solution.py:241
  17.3 0.1 compare_select_fusion
  17.4 0.1 reshape.158
  17.5 0.8 %gather_fusion = f32[64]{0:T(128)S(1)} fusion(f32[256]{0:T(256)S(1)} %copy-done, s32[1024]{0:T(1024)S(1)} %pad_clamp_fusion), kind=kCustom, calls=%fused_computation | custom fusion | bytes 768 | tf_op jit(solution)/shard_map/jit(_take)/gather | solution.py:259
  18.3 0.1 reshape.157
  18.4 0.1 and_select_fusion
  18.5 0.1 iota_add_fusion
  18.5 0.7 %copy-done.8 = f32[2]{0:T(128)S(1)} copy-done((f32[2]{0:T(128)S(1)}, f32[2]{0:T(128)}, u32[]{:S(2)}) %copy-start.8) | copy-done | bytes 32
  19.2 0.7 %copy-done.7 = s32[4]{0:T(128)S(1)} copy-done((s32[4]{0:T(128)S(1)}, s32[4]{0:T(128)}, u32[]{:S(2)}) %copy-start.7) | copy-done | bytes 40
  19.8 0.1 broadcast_compare_fusion
  19.9 0.6 %copy-done.6 = f32[4]{0:T(128)S(1)} copy-done((f32[4]{0:T(128)S(1)}, f32[4]{0:T(128)}, u32[]{:S(2)}) %copy-start.6) | copy-done | bytes 40
  20.5 0.1 subtract_multiply_fusion.1
  20.6 7.9 %all-to-all-done = bf16[16,16,512]{2,1,0:T(8,128)(2,1)S(1)} async-done(((bf16[16,16,512]{2,1,0:T(8,128)(2,1)}), bf16[16,16,512]{2,1,0:T(8,128)(2,1)S(1)}, u32[]{:S(2)}, u32[]{:S(2)}) %all-to-all-start) | async-done | bytes 262176 | tf_op jit(solution)/shard_map/all_to_all | solution.py:241
  28.6 0.6 %collective-permute-start = (bf16[128,640]{1,0:T(8,128)(2,1)S(1)}, bf16[128,640]{1,0:T(8,128)(2,1)S(1)}, u32[]{:S(2)}, u32[]{:S(2)}) collective-permute-start(bf16[128,640]{1,0:T(8,128)(2,1)S(1)} %get-tuple-element.16), channel_id=1, source_target_pairs={{0,64},{1,17},{2,66},{3,19},{4,68},{5,21},{6,70},{7,23},{8,72},{9,... | collective-permute-start | bytes 491528 | tf_op jit(solution)/shard_map/ppermute | solution.py:255
  29.2 2.4 %collective-permute-start.1 = (bf16[128,640]{1,0:T(8,128)(2,1)S(1)}, bf16[128,640]{1,0:T(8,128)(2,1)S(1)}, u32[]{:S(2)}, u32[]{:S(2)}) collective-permute-start(bf16[128,640]{1,0:T(8,128)(2,1)S(1)} %get-tuple-element.17), channel_id=1, source_target_pairs={{0,128},{1,33},{2,130},{3,35},{4,132},{5,37},{6,134},{7,39},{8,136... | collective-permute-start | bytes 491528 | tf_op jit(solution)/shard_map/ppermute | solution.py:255
  31.6 0.3 select_multiply_fusion
  31.9 2.1 %collective-permute-done.one = bf16[128,640]{1,0:T(8,128)(2,1)S(1)} collective-permute-done((bf16[128,640]{1,0:T(8,128)(2,1)S(1)}, bf16[128,640]{1,0:T(8,128)(2,1)S(1)}, u32[]{:S(2)}, u32[]{:S(2)}) %collective-permute-start) | collective-permute-done | bytes 163872 | tf_op jit(solution)/shard_map/ppermute | solution.py:255
  34.0 2.0 %collective-permute-done.1.two = bf16[128,640]{1,0:T(8,128)(2,1)S(1)} collective-permute-done((bf16[128,640]{1,0:T(8,128)(2,1)S(1)}, bf16[128,640]{1,0:T(8,128)(2,1)S(1)}, u32[]{:S(2)}, u32[]{:S(2)}) %collective-permute-start.1) | collective-permute-done | bytes 163872 | tf_op jit(solution)/shard_map/ppermute | solution.py:255
  36.0 2.1 %collective-permute-done.2.three = bf16[128,640]{1,0:T(8,128)(2,1)S(1)} collective-permute-done((bf16[128,640]{1,0:T(8,128)(2,1)S(1)}, bf16[128,640]{1,0:T(8,128)(2,1)S(1)}, u32[]{:S(2)}, u32[]{:S(2)}) %collective-permute-start.2) | collective-permute-done | bytes 163872 | tf_op jit(solution)/shard_map/ppermute | solution.py:255
  38.2 0.8 %product.1 = (f32[128,512]{1,0:T(8,128)S(1)}, bf16[128,512]{1,0:T(8,128)(2,1)S(1)}, bf16[128,512]{1,0:T(8,128)(2,1)S(1)}, bf16[128,512]{1,0:T(8,128)(2,1)S(1)}) custom-call(s32[1]{0:T(128)} %bitcast.turn, f32[4,128,2]{2,1,0:T(8,128)S(1)} %bitcast.20, bf16[128,640]{1,0:T(8,128)(2,1)S(1)} %get-tuple-element.18.own, ...), custom_call_target="tpu_custom_call" | custom-call | flops 300000000 | bytes 2000000 | tf_op jit(solution)/shard_map/product/pallas_call | solution.py:209
  39.0 1.7 %collective-permute-start.3 = (bf16[128,512]{1,0:T(8,128)(2,1)S(1)}, bf16[128,512]{1,0:T(8,128)(2,1)S(1)}, u32[]{:S(2)}, u32[]{:S(2)}) collective-permute-start(bf16[128,512]{1,0:T(8,128)(2,1)S(1)} %get-tuple-element.10), channel_id=1, source_target_pairs={{0,16},{1,65},{2,18},{3,67},{4,20},{5,69},{6,22},{7,71},{8,24},{9,... | collective-permute-start | bytes 393224 | tf_op jit(solution)/shard_map/ppermute | solution.py:269
  40.6 1.7 %collective-permute-start.4 = (bf16[128,512]{1,0:T(8,128)(2,1)S(1)}, bf16[128,512]{1,0:T(8,128)(2,1)S(1)}, u32[]{:S(2)}, u32[]{:S(2)}) collective-permute-start(bf16[128,512]{1,0:T(8,128)(2,1)S(1)} %get-tuple-element.11), channel_id=1, source_target_pairs={{0,48},{1,193},{2,50},{3,195},{4,52},{5,197},{6,54},{7,199},{8,56}... | collective-permute-start | bytes 393224 | tf_op jit(solution)/shard_map/ppermute | solution.py:269
  42.3 2.0 %collective-permute-start.5 = (bf16[128,512]{1,0:T(8,128)(2,1)S(1)}, bf16[128,512]{1,0:T(8,128)(2,1)S(1)}, u32[]{:S(2)}, u32[]{:S(2)}) collective-permute-start(bf16[128,512]{1,0:T(8,128)(2,1)S(1)} %get-tuple-element.12), channel_id=1, source_target_pairs={{0,32},{1,129},{2,34},{3,131},{4,36},{5,133},{6,38},{7,135},{8,40}... | collective-permute-start | bytes 393224 | tf_op jit(solution)/shard_map/ppermute | solution.py:269
  44.3 1.0 %collective-permute-done.3 = bf16[128,512]{1,0:T(8,128)(2,1)S(1)} collective-permute-done((bf16[128,512]{1,0:T(8,128)(2,1)S(1)}, bf16[128,512]{1,0:T(8,128)(2,1)S(1)}, u32[]{:S(2)}, u32[]{:S(2)}) %collective-permute-start.3) | collective-permute-done | bytes 131104 | tf_op jit(solution)/shard_map/ppermute | solution.py:269
  45.3 0.4 collective-permute-done.4
  45.6 3.2 %collective-permute-done.5 = bf16[128,512]{1,0:T(8,128)(2,1)S(1)} collective-permute-done((bf16[128,512]{1,0:T(8,128)(2,1)S(1)}, bf16[128,512]{1,0:T(8,128)(2,1)S(1)}, u32[]{:S(2)}, u32[]{:S(2)}) %collective-permute-start.5) | collective-permute-done | bytes 131104 | tf_op jit(solution)/shard_map/ppermute | solution.py:269
  48.8 0.8 %copy.18 = bf16[2,2,32,512]{3,1,0,2:T(2,128)(2,1)} copy(bf16[2,2,32,512]{3,2,1,0:T(8,128)(2,1)S(1)} %bitcast.24) | data formatting | bytes 262144 | tf_op jit(solution)/shard_map/convert_element_type | solution.py:270
  (22 shorter events, 0.4 us)
Async XLA Ops:
  0.0 17.5 %copy-start = (f32[256]{0:T(256)S(1)}, f32[256]{0:T(256)}, u32[]{:S(2)}) copy-start(f32[256]{0:T(256)} %param.13) | copy-start | bytes 3076
  0.0 1.6 %copy-start.5 = (bf16[4,110592]{1,0:T(4,128)(2,1)S(1)}, bf16[4,110592]{1,0:T(4,128)(2,1)}, u32[]{:S(2)}) copy-start(bf16[4,110592]{1,0:T(4,128)(2,1)} %param.10) | copy-start | bytes 2654212
  1.6 0.7 %copy-start.1 = (s32[2048]{0:T(1024)S(1)}, s32[2048]{0:T(1024)}, u32[]{:S(2)}) copy-start(s32[2048]{0:T(1024)} %param.15) | copy-start | bytes 24580
  1.6 1.0 %copy-start.2 = (bf16[2,400,256]{2,1,0:T(8,128)(2,1)S(1)}, bf16[2,400,256]{2,1,0:T(8,128)(2,1)}, u32[]{:S(2)}) copy-start(bf16[2,400,256]{2,1,0:T(8,128)(2,1)} %constant.71.clone.first) | copy-start | bytes 1228804
  1.6 1.0 %copy-start.3 = (bf16[384,256]{1,0:T(8,128)(2,1)S(1)}, bf16[384,256]{1,0:T(8,128)(2,1)}, u32[]{:S(2)}) copy-start(bf16[384,256]{1,0:T(8,128)(2,1)} %constant.73.clone.third) | copy-start | bytes 589828
  1.6 1.1 %copy-start.4 = (bf16[192,192]{1,0:T(8,128)(2,1)S(1)}, bf16[192,192]{1,0:T(8,128)(2,1)}, u32[]{:S(2)}) copy-start(bf16[192,192]{1,0:T(8,128)(2,1)} %constant.72.clone.second) | copy-start | bytes 221188
  8.7 19.8 %all-to-all-start = ((bf16[16,16,512]{2,1,0:T(8,128)(2,1)}), bf16[16,16,512]{2,1,0:T(8,128)(2,1)S(1)}, u32[]{:S(2)}, u32[]{:S(2)}) async-start(bf16[16,16,512]{2,1,0:T(8,128)(2,1)} %bitcast.3), calls=%async_computation | async-start | bytes 524288 | tf_op jit(solution)/shard_map/all_to_all | solution.py:241
  18.5 0.7 %copy-start.8 = (f32[2]{0:T(128)S(1)}, f32[2]{0:T(128)}, u32[]{:S(2)}) copy-start(f32[2]{0:T(128)} %param.14) | copy-start | bytes 28
  19.2 0.7 %copy-start.7 = (s32[4]{0:T(128)S(1)}, s32[4]{0:T(128)}, u32[]{:S(2)}) copy-start(s32[4]{0:T(128)} %param.16) | copy-start | bytes 52
  19.8 0.7 %copy-start.6 = (f32[4]{0:T(128)S(1)}, f32[4]{0:T(128)}, u32[]{:S(2)}) copy-start(f32[4]{0:T(128)} %param.12) | copy-start | bytes 52
  28.6 5.4 %collective-permute-start = (bf16[128,640]{1,0:T(8,128)(2,1)S(1)}, bf16[128,640]{1,0:T(8,128)(2,1)S(1)}, u32[]{:S(2)}, u32[]{:S(2)}) collective-permute-start(bf16[128,640]{1,0:T(8,128)(2,1)S(1)} %get-tuple-element.16), channel_id=1, source_target_pairs={{0,64},{1,17},{2,66},{3,19},{4,68},{5,21},{6,70},{7,23},{8,72},{9,... | collective-permute-start | bytes 491528 | tf_op jit(solution)/shard_map/ppermute | solution.py:255
  29.2 6.8 %collective-permute-start.1 = (bf16[128,640]{1,0:T(8,128)(2,1)S(1)}, bf16[128,640]{1,0:T(8,128)(2,1)S(1)}, u32[]{:S(2)}, u32[]{:S(2)}) collective-permute-start(bf16[128,640]{1,0:T(8,128)(2,1)S(1)} %get-tuple-element.17), channel_id=1, source_target_pairs={{0,128},{1,33},{2,130},{3,35},{4,132},{5,37},{6,134},{7,39},{8,136... | collective-permute-start | bytes 491528 | tf_op jit(solution)/shard_map/ppermute | solution.py:255
  31.6 6.5 %collective-permute-start.2 = (bf16[128,640]{1,0:T(8,128)(2,1)S(1)}, bf16[128,640]{1,0:T(8,128)(2,1)S(1)}, u32[]{:S(2)}, u32[]{:S(2)}) collective-permute-start(bf16[128,640]{1,0:T(8,128)(2,1)S(1)} %get-tuple-element.15), channel_id=1, source_target_pairs={{0,192},{1,49},{2,194},{3,51},{4,196},{5,53},{6,198},{7,55},{8,200... | collective-permute-start | bytes 491528 | tf_op jit(solution)/shard_map/ppermute | solution.py:255
  39.0 6.3 %collective-permute-start.3 = (bf16[128,512]{1,0:T(8,128)(2,1)S(1)}, bf16[128,512]{1,0:T(8,128)(2,1)S(1)}, u32[]{:S(2)}, u32[]{:S(2)}) collective-permute-start(bf16[128,512]{1,0:T(8,128)(2,1)S(1)} %get-tuple-element.10), channel_id=1, source_target_pairs={{0,16},{1,65},{2,18},{3,67},{4,20},{5,69},{6,22},{7,71},{8,24},{9,... | collective-permute-start | bytes 393224 | tf_op jit(solution)/shard_map/ppermute | solution.py:269
  40.6 5.0 %collective-permute-start.4 = (bf16[128,512]{1,0:T(8,128)(2,1)S(1)}, bf16[128,512]{1,0:T(8,128)(2,1)S(1)}, u32[]{:S(2)}, u32[]{:S(2)}) collective-permute-start(bf16[128,512]{1,0:T(8,128)(2,1)S(1)} %get-tuple-element.11), channel_id=1, source_target_pairs={{0,48},{1,193},{2,50},{3,195},{4,52},{5,197},{6,54},{7,199},{8,56}... | collective-permute-start | bytes 393224 | tf_op jit(solution)/shard_map/ppermute | solution.py:269
  42.3 6.5 %collective-permute-start.5 = (bf16[128,512]{1,0:T(8,128)(2,1)S(1)}, bf16[128,512]{1,0:T(8,128)(2,1)S(1)}, u32[]{:S(2)}, u32[]{:S(2)}) collective-permute-start(bf16[128,512]{1,0:T(8,128)(2,1)S(1)} %get-tuple-element.12), channel_id=1, source_target_pairs={{0,32},{1,129},{2,34},{3,131},{4,36},{5,133},{6,38},{7,135},{8,40}... | collective-permute-start | bytes 393224 | tf_op jit(solution)/shard_map/ppermute | solution.py:269

commit v2 on v1

--- a/solution.py
+++ b/solution.py
@@ -70,6 +70,23 @@
 def split(value):
     high = value.astype(BF)
     return high, (value - high.astype(jnp.float32)).astype(BF)
+
+
+MEMBERS = (((0, 1), (2, 3)), ((0, 3), (1, 2)))
+
+
+def reduce_order(tiles, quarter, kind):
+    result = []
+    for xs in MEMBERS[kind]:
+        for ys in MEMBERS[kind]:
+            made = None
+            for n in range(4):
+                x, y = xs[n // 2], ys[n % 2]
+                shift = 32 * (n - y) % 128
+                moved = pltpu.roll(tiles[x], shift, 1) if shift else tiles[x]
+                made = moved if made is None else jnp.where(quarter == n, moved, made)
+            result.append(made)
+    return jnp.concatenate(result, 1)
 
 
 def density_kernel(cond, val, gvec, first, second, third, out, xh, xl, u, yh, yl, z, dens):
@@ -138,15 +155,7 @@
     quarter = lax.broadcasted_iota(jnp.int32, (8, 128), 1) // 32
     for i in range(4):
         tiles = [dens[:, 512 * i + 128 * t : 512 * i + 128 * t + 128] for t in range(4)]
-        turned = []
-        for t in range(4):
-            tile = tiles[t]
-            for other in range(4):
-                if other != t:
-                    moved = pltpu.roll(tiles[other], (32 * (other - t)) % 128, 1)
-                    tile = jnp.where(quarter == other, moved, tile)
-            turned.append(tile)
-        orders = (jnp.concatenate(tiles, 1), jnp.concatenate(turned, 1))
+        orders = [reduce_order(tiles, quarter, kind) for kind in (1, 0)]
         for j in range(4):
             at = 16 * (4 * i + j)
             both = jnp.concatenate([dens[:, 512 * j : 512 * j + 512], orders[j % 2]], 0)
@@ -179,28 +188,26 @@
 
 
 def product_kernel(turn, weight, own, one, two, three, mine, first, second, third):
-    cols, lefts = [], []
-    for n, block in enumerate((own, one, two, three)):
-        cols.append(block[:, :512])
-        rows = block[:, 512:640].astype(jnp.float32)
-        rows = pltpu.roll(rows, lax.rem(128 - 32 * turn[0], 128), 1)
-        split_rows = rows.reshape(16, 2, 4, 128)
-        swapped = jnp.concatenate([split_rows[:, 1:], -split_rows[:, :1]], 1).reshape(128, 128)
-        parts = []
-        for freq in range(2):
-            scale = weight[n, :, freq : freq + 1]
-            parts.append((scale * rows).astype(BF))
-            parts.append((scale * swapped).astype(BF))
-        lefts.append(jnp.concatenate(parts, 1))
-    left = jnp.concatenate(lefts, 0)
-    right = jnp.concatenate(cols, 0)
+    blocks = (own, one, two, three)
+    twice = []
+    for block in blocks:
+        rows = block[:, 512:640]
+        parts = rows.astype(jnp.float32).reshape(16, 2, 4, 128)
+        swapped = jnp.concatenate([parts[:, 1:], -parts[:, :1]], 1).reshape(128, 128)
+        twice.append(jnp.concatenate([rows, swapped.astype(BF)], 1))
+    lane = lax.broadcasted_iota(jnp.int32, (256, 512), 1)
+    spot = ((lane // 128) ^ turn[0]) * 32 + (lane // 4) % 32 + 128 * (lane % 2)
+    copies = jnp.where(lax.broadcasted_iota(jnp.int32, (256, 512), 0) == spot, 1.0, 0.0).astype(BF)
+    spread = dot_nn(jnp.concatenate(twice, 0), copies)
+    scale = weight[...].reshape(512, 2)
+    early = (lax.broadcasted_iota(jnp.int32, (512, 512), 1) // 2) % 2 == 0
+    left = (jnp.where(early, scale[:, 0:1], scale[:, 1:2]) * spread).astype(BF)
+    right = jnp.concatenate([block[:, :512] for block in blocks], 0)
     total = lax.dot_general(left, right, (((0,), (0,)), ((), ())), preferred_element_type=jnp.float32)
-    for part in range(4):
-        at = 128 * part
-        mine[32 * part : 32 * part + 32, :] = total[at : at + 32]
-        first[32 * part : 32 * part + 32, :] = total[at + 32 : at + 64].astype(BF)
-        second[32 * part : 32 * part + 32, :] = total[at + 64 : at + 96].astype(BF)
-        third[32 * part : 32 * part + 32, :] = total[at + 96 : at + 128].astype(BF)
+    mine[...] = total[:128]
+    first[...] = total[128:256].astype(BF)
+    second[...] = total[256:384].astype(BF)
+    third[...] = total[384:].astype(BF)
 
 
 def product_call(turn, weight, blocks):
@@ -217,17 +224,40 @@
     )(turn, weight, *blocks)
 
 
-def ring_pairs(across, along, rest, step, gather):
+def sum_kernel(mine, first, second, third, out):
+    total = mine[...]
+    for piece in (first, second, third):
+        total = total + piece[...].astype(jnp.float32)
+    out[...] = total.reshape(out.shape).astype(BF)
+
+
+def sum_call(mine, pieces, shape):
+    vmem = pl.BlockSpec(memory_space=pltpu.VMEM)
+    return pl.pallas_call(
+        sum_kernel,
+        out_shape=jax.ShapeDtypeStruct(shape, BF),
+        in_specs=[vmem] * 4,
+        out_specs=vmem,
+        name="add",
+    )(mine, *pieces)
+
+
+def exchange(block, step, gather):
+    across, along = lax.axis_size("bx"), lax.axis_size("by")
+    rest = lax.axis_size("grow") * lax.axis_size("zlo") * lax.axis_size("core")
+
+    def partner(place, kind):
+        return 3 - place if kind else place ^ 1
+
     pairs = []
     for x in range(across):
         for y in range(along):
             for z in range(rest):
-                if (z % 2 == 0) == gather:
-                    to = ((x + step) % across, y)
-                else:
-                    to = (x, (y + step) % along)
-                pairs.append(((x * along + y) * rest + z, (to[0] * along + to[1]) * rest + z))
-    return pairs
+                kind = z % 2 if gather else 1 - z % 2
+                to_x = partner(x, kind) if step // 2 else x
+                to_y = partner(y, kind) if step % 2 else y
+                pairs.append(((x * along + y) * rest + z, (to_x * along + to_y) * rest + z))
+    return lax.ppermute(block, ALL, pairs)
 
 
 def on_device(valence, conduction, val_energy, cond_energy, frequencies, gvec_index, first_band):
@@ -244,17 +274,24 @@
     x_here = lax.axis_index("bx")
     y_here = lax.axis_index("by")
     even = lax.axis_index("core") == 0
-    place = jnp.where(even, x_here, y_here)
-    other = jnp.where(even, y_here, x_here)
+
+    def tile_of(place):
+        return jnp.where(even, (place ^ (place >> 1)) & 1, place >> 1)
+
+    def spot_of(place):
+        return jnp.where(even, place >> 1, place & 1)
+
+    tile = 2 * tile_of(x_here) + tile_of(y_here)
+    spot = 2 * spot_of(x_here) + spot_of(y_here)
     blocks = {}
-    for step in (0, 1, 3, 2):
-        target = lax.rem(place + step, across)
-        part = lax.dynamic_slice_in_dim(rows, target * 128, 128, 1)
+    for step in (0, 3, 2, 1):
+        part = lax.dynamic_slice_in_dim(rows, (tile ^ step) * 128, 128, 1)
         block = jnp.concatenate([cols, part], 1)
-        pairs = ring_pairs(across, along, group, step, True)
-        blocks[step] = lax.ppermute(block, ALL, pairs) if step else block
-    source = lax.rem(place - jnp.arange(across, dtype=jnp.int32) + across, across)
-    band = jnp.where(even, source * along + other, other * along + source)
+        blocks[step] = exchange(block, step, True) if step else block
+    steps = jnp.arange(4, dtype=jnp.int32)
+    x_from = jnp.where(steps // 2 == 0, x_here, jnp.where(even, x_here ^ 1, 3 - x_here))
+    y_from = jnp.where(steps % 2 == 0, y_here, jnp.where(even, y_here ^ 1, 3 - y_here))
+    band = x_from * along + y_from
     bands = (band * group)[:, None] + jnp.arange(group, dtype=jnp.int32)
     energies = jnp.take(cond_energy, bands)
     gap = energies[..., None] - val_energy
@@ -263,11 +300,9 @@
     weight = jnp.where(counted[..., None], ratio, 0.0) / (cond_energy.shape[0] * num_val)
     weight = jnp.broadcast_to(weight[:, :, None], (across, group, 2, num_val, frequencies.shape[0]))
     weight = weight.reshape(across, group * lines, frequencies.shape[0])
-    total, *pieces = product_call(other.reshape(1), weight, [blocks[step] for step in range(across)])
-    for step in (1, 3, 2):
-        pairs = ring_pairs(across, along, group, step, False)
-        total = total + lax.ppermute(pieces[step - 1], ALL, pairs).astype(jnp.float32)
-    return jnp.transpose(total.reshape(2, 2, 32, 512), (2, 0, 1, 3)).astype(BF)
+    total, *pieces = product_call(spot.reshape(1), weight, [blocks[step] for step in range(4)])
+    pieces = [exchange(pieces[step - 1], step, False) for step in (3, 2, 1)]
+    return sum_call(total, pieces, (32, frequencies.shape[0], 2, 512))
 
 
 def solution(mesh):

time: 50.2 us -> 54.1 us (1.078)
  Pallas kernels: 6.85 us -> 8.69 us
  starting transfers between devices: 16.8 us -> 18.1 us
  local copies, waits for them, and re-layouts: 6.38 us -> 6.95 us
    pallas_call x0 -> x1, Pallas kernels: none -> 1.94 us  [sum_call(): pl.pallas_call(sum_kernel, out_shape=jax.ShapeDtypeStruct(shape, BF), in_...]
    unnamed x18 -> x26, local copies, waits for them, and re-layouts: 2.82 us -> 4.18 us
    ppermute x6, starting transfers between devices: 8.27 us -> 9.48 us  [exchange(): return lax.ppermute(block, ALL, pairs)]
    convert_element_type x1 -> x0, local copies, waits for them, and re-layouts: 0.79 us -> none  [on_device(): return jnp.transpose(total.reshape(2, 2, 32, 512), (2, 0, 1, 3)).astype(BF)]
where the time goes in v2:
time: 54.1 us; the launch traced here: 53.2 us
  waiting for transfers between devices  18.6 us (34%)
  starting transfers between devices  18.1 us (33%)
  Pallas kernels  8.69 us (16%)
  local copies, waits for them, and re-layouts  6.95 us (13%)
  other arithmetic  0.71 us (1%)
    ppermute x6, waiting for transfers between devices, exchange(): return lax.ppermute(block, ALL, pairs)  10.7 us
    ppermute x6, starting transfers between devices, exchange(): return lax.ppermute(block, ALL, pairs)  9.48 us
    all_to_all x1, starting transfers between devices, on_device(): got = lax.all_to_all(sent, ZED, split_axis=0, concat_axis=0, tiled=True)  8.57 us
    all_to_all x1, waiting for transfers between devices, on_device(): got = lax.all_to_all(sent, ZED, split_axis=0, concat_axis=0, tiled=True)  7.9 us
    pallas_call x1, Pallas kernels, density_call(): pl.pallas_call(density_kernel, out_shape=jax.ShapeDtypeStruct((256, 512),...  6.02 us
    unnamed x26, local copies, waits for them, and re-layouts  4.18 us
    pallas_call x1, Pallas kernels, sum_call(): pl.pallas_call(sum_kernel, out_shape=jax.ShapeDtypeStruct(shape, BF), in_...  1.94 us
    pad x1, local copies, waits for them, and re-layouts, density_call(): cond = jnp.pad(conduction, ((0, 3), (0, 0))).reshape(4, GRID, GRID * GRID)  1.55 us
  transfers between devices with their start and end apart: 7, of which 7 were waited for; matrix products, arithmetic and copies ran while one was open for 3% of the time, Pallas kernels for 0%

profile of v2, /device:TPU:6, one launch (start us, length us, event | category | flops | bytes accessed | tf_op | source)
XLA Modules:
  0.0 53.2 jit_solution(15335817619508396123)
XLA Ops:
  0.0 1.5 %pad.4 = bf16[4,110592]{1,0:T(4,128)(2,1)S(1)} pad(bf16[1,110592]{1,0:T(2,128)(2,1)} %param.11, bf16[]{:T(256)} %constant.83.clone.1), padding=0_3x0_0 | pad | bytes 1105922 | tf_op jit(solution)/shard_map/jit(_pad)/pad | solution.py:167
  1.6 0.2 copy_bitcast_fusion
  1.8 0.5 copy-done.2
  2.3 0.3 copy-done.3
  2.7 6.0 %density.1 = bf16[256,512]{1,0:T(8,128)(2,1)} custom-call(bf16[4,48,2304]{2,1,0:T(8,128)(2,1)S(1)} %get-tuple-element.26.cond, bf16[4,48,2304]{2,1,0:T(8,128)(2,1)S(1)} %get-tuple-element.25.val, s32[1,2048]{1,0:T(1,128)S(1)} %bitcast.17, bf16[2,400,256]{2,1,0:T(8,128)(2,1)S(1)} %copy-done.3, bf16[192,192]{1,0:T(8,128)(2,1)S(1)} %copy-done.5, ...), custom_call_target="tpu_custom_call" | custom-call | flops 5000000000 | bytes 3000000 | tf_op jit(solution)/shard_map/density/pallas_call | solution.py:170
  8.7 8.6 %all-to-all-start = ((bf16[16,16,512]{2,1,0:T(8,128)(2,1)}), bf16[16,16,512]{2,1,0:T(8,128)(2,1)S(1)}, u32[]{:S(2)}, u32[]{:S(2)}) async-start(bf16[16,16,512]{2,1,0:T(8,128)(2,1)} %bitcast.3), calls=%async_computation | async-start | bytes 524288 | tf_op jit(solution)/shard_map/all_to_all | solution.py:271
  17.4 0.1 reshape.167
  17.5 0.8 %gather_fusion = f32[64]{0:T(128)S(1)} fusion(f32[256]{0:T(256)S(1)} %copy-done, s32[1024]{0:T(1024)S(1)} %pad_clamp_fusion), kind=kCustom, calls=%fused_computation | custom fusion | bytes 768 | tf_op jit(solution)/shard_map/jit(_take)/gather | solution.py:296
  18.3 0.1 reshape.166
  18.4 0.1 and_select_fusion
  18.5 0.7 %copy-done.12 = f32[2]{0:T(128)S(1)} copy-done((f32[2]{0:T(128)S(1)}, f32[2]{0:T(128)}, u32[]{:S(2)}) %copy-start.12) | copy-done | bytes 32
  19.2 0.7 %copy-done.11 = s32[4]{0:T(128)S(1)} copy-done((s32[4]{0:T(128)S(1)}, s32[4]{0:T(128)}, u32[]{:S(2)}) %copy-start.11) | copy-done | bytes 40
  19.9 0.1 broadcast_compare_fusion
  19.9 0.6 %copy-done.10 = f32[4]{0:T(128)S(1)} copy-done((f32[4]{0:T(128)S(1)}, f32[4]{0:T(128)}, u32[]{:S(2)}) %copy-start.10) | copy-done | bytes 40
  20.6 7.9 %all-to-all-done = bf16[16,16,512]{2,1,0:T(8,128)(2,1)S(1)} async-done(((bf16[16,16,512]{2,1,0:T(8,128)(2,1)}), bf16[16,16,512]{2,1,0:T(8,128)(2,1)S(1)}, u32[]{:S(2)}, u32[]{:S(2)}) %all-to-all-start) | async-done | bytes 262176 | tf_op jit(solution)/shard_map/all_to_all | solution.py:271
  28.6 1.7 %collective-permute-start = (bf16[128,640]{1,0:T(8,128)(2,1)S(1)}, bf16[128,640]{1,0:T(8,128)(2,1)S(1)}, u32[]{:S(2)}, u32[]{:S(2)}) collective-permute-start(bf16[128,640]{1,0:T(8,128)(2,1)S(1)} %get-tuple-element.16), channel_id=1, source_target_pairs={{0,16},{1,49},{2,18},{3,51},{4,20},{5,53},{6,22},{7,55},{8,24},{9,... | collective-permute-start | bytes 491528 | tf_op jit(solution)/shard_map/ppermute | solution.py:260
  30.3 0.8 %collective-permute-start.1 = (bf16[128,640]{1,0:T(8,128)(2,1)S(1)}, bf16[128,640]{1,0:T(8,128)(2,1)S(1)}, u32[]{:S(2)}, u32[]{:S(2)}) collective-permute-start(bf16[128,640]{1,0:T(8,128)(2,1)S(1)} %get-tuple-element.17), channel_id=1, source_target_pairs={{0,64},{1,193},{2,66},{3,195},{4,68},{5,197},{6,70},{7,199},{8,72}... | collective-permute-start | bytes 491528 | tf_op jit(solution)/shard_map/ppermute | solution.py:260
  31.1 1.1 %collective-permute-start.2 = (bf16[128,640]{1,0:T(8,128)(2,1)S(1)}, bf16[128,640]{1,0:T(8,128)(2,1)S(1)}, u32[]{:S(2)}, u32[]{:S(2)}) collective-permute-start(bf16[128,640]{1,0:T(8,128)(2,1)S(1)} %get-tuple-element.15), channel_id=1, source_target_pairs={{0,80},{1,241},{2,82},{3,243},{4,84},{5,245},{6,86},{7,247},{8,88}... | collective-permute-start | bytes 491528 | tf_op jit(solution)/shard_map/ppermute | solution.py:260
  32.2 0.3 select_multiply_fusion
  32.5 1.6 %collective-permute-done.one = bf16[128,640]{1,0:T(8,128)(2,1)S(1)} collective-permute-done((bf16[128,640]{1,0:T(8,128)(2,1)S(1)}, bf16[128,640]{1,0:T(8,128)(2,1)S(1)}, u32[]{:S(2)}, u32[]{:S(2)}) %collective-permute-start) | collective-permute-done | bytes 163872 | tf_op jit(solution)/shard_map/ppermute | solution.py:260
  34.0 1.6 %collective-permute-done.1.two = bf16[128,640]{1,0:T(8,128)(2,1)S(1)} collective-permute-done((bf16[128,640]{1,0:T(8,128)(2,1)S(1)}, bf16[128,640]{1,0:T(8,128)(2,1)S(1)}, u32[]{:S(2)}, u32[]{:S(2)}) %collective-permute-start.1) | collective-permute-done | bytes 163872 | tf_op jit(solution)/shard_map/ppermute | solution.py:260
  35.6 1.7 %collective-permute-done.2.three = bf16[128,640]{1,0:T(8,128)(2,1)S(1)} collective-permute-done((bf16[128,640]{1,0:T(8,128)(2,1)S(1)}, bf16[128,640]{1,0:T(8,128)(2,1)S(1)}, u32[]{:S(2)}, u32[]{:S(2)}) %collective-permute-start.2) | collective-permute-done | bytes 163872 | tf_op jit(solution)/shard_map/ppermute | solution.py:260
  37.4 0.7 %product.1 = (f32[128,512]{1,0:T(8,128)S(1)}, bf16[128,512]{1,0:T(8,128)(2,1)S(1)}, bf16[128,512]{1,0:T(8,128)(2,1)S(1)}, bf16[128,512]{1,0:T(8,128)(2,1)S(1)}) custom-call(s32[1]{0:T(128)} %bitcast.turn, f32[4,128,2]{2,1,0:T(8,128)S(1)} %bitcast.16, bf16[128,640]{1,0:T(8,128)(2,1)S(1)} %get-tuple-element.18.own, ...), custom_call_target="tpu_custom_call" | custom-call | flops 300000000 | bytes 2000000 | tf_op jit(solution)/shard_map/product/pallas_call | solution.py:216
  38.1 0.7 %copy-done.1 = f32[128,512]{1,0:T(8,128)} copy-done((f32[128,512]{1,0:T(8,128)}, f32[128,512]{1,0:T(8,128)S(1)}, u32[]{:S(2)}) %copy-start.1) | copy-done | bytes 262168
  38.8 2.8 %collective-permute-start.3 = (bf16[128,512]{1,0:T(8,128)(2,1)S(1)}, bf16[128,512]{1,0:T(8,128)(2,1)S(1)}, u32[]{:S(2)}, u32[]{:S(2)}) collective-permute-start(bf16[128,512]{1,0:T(8,128)(2,1)S(1)} %get-tuple-element.10), channel_id=1, source_target_pairs={{0,240},{1,81},{2,242},{3,83},{4,244},{5,85},{6,246},{7,87},{8,248... | collective-permute-start | bytes 393224 | tf_op jit(solution)/shard_map/ppermute | solution.py:260
  41.7 2.8 %collective-permute-start.4 = (bf16[128,512]{1,0:T(8,128)(2,1)S(1)}, bf16[128,512]{1,0:T(8,128)(2,1)S(1)}, u32[]{:S(2)}, u32[]{:S(2)}) collective-permute-start(bf16[128,512]{1,0:T(8,128)(2,1)S(1)} %get-tuple-element.11), channel_id=1, source_target_pairs={{0,192},{1,65},{2,194},{3,67},{4,196},{5,69},{6,198},{7,71},{8,200... | collective-permute-start | bytes 393224 | tf_op jit(solution)/shard_map/ppermute | solution.py:260
  44.4 0.3 collective-permute-start.5
  44.7 2.4 %collective-permute-done.3.first = bf16[128,512]{1,0:T(8,128)(2,1)S(1)} collective-permute-done((bf16[128,512]{1,0:T(8,128)(2,1)S(1)}, bf16[128,512]{1,0:T(8,128)(2,1)S(1)}, u32[]{:S(2)}, u32[]{:S(2)}) %collective-permute-start.3) | collective-permute-done | bytes 131104 | tf_op jit(solution)/shard_map/ppermute | solution.py:260
  47.1 1.7 %collective-permute-done.4.second = bf16[128,512]{1,0:T(8,128)(2,1)S(1)} collective-permute-done((bf16[128,512]{1,0:T(8,128)(2,1)S(1)}, bf16[128,512]{1,0:T(8,128)(2,1)S(1)}, u32[]{:S(2)}, u32[]{:S(2)}) %collective-permute-start.4) | collective-permute-done | bytes 131104 | tf_op jit(solution)/shard_map/ppermute | solution.py:260
  48.8 1.8 %collective-permute-done.5.third = bf16[128,512]{1,0:T(8,128)(2,1)S(1)} collective-permute-done((bf16[128,512]{1,0:T(8,128)(2,1)S(1)}, bf16[128,512]{1,0:T(8,128)(2,1)S(1)}, u32[]{:S(2)}, u32[]{:S(2)}) %collective-permute-start.5) | collective-permute-done | bytes 131104 | tf_op jit(solution)/shard_map/ppermute | solution.py:260
  50.6 0.7 %copy-done.9 = bf16[128,512]{1,0:T(8,128)(2,1)} copy-done((bf16[128,512]{1,0:T(8,128)(2,1)}, bf16[128,512]{1,0:T(8,128)(2,1)S(1)}, u32[]{:S(2)}) %copy-start.9) | copy-done | bytes 131096
  51.3 1.9 %add.170 = bf16[32,2,2,512]{3,2,1,0:T(2,128)(2,1)} custom-call(f32[128,512]{1,0:T(8,128)} %copy-done.1, bf16[128,512]{1,0:T(8,128)(2,1)} %copy-done.7, bf16[128,512]{1,0:T(8,128)(2,1)} %copy-done.8, bf16[128,512]{1,0:T(8,128)(2,1)} %copy-done.9), custom_call_target="tpu_custom_call" | custom-call | tf_op jit(solution)/shard_map/add/pallas_call | solution.py:236
  (29 shorter events, 0.5 us)
Async XLA Ops:
  0.0 17.5 %copy-start = (f32[256]{0:T(256)S(1)}, f32[256]{0:T(256)}, u32[]{:S(2)}) copy-start(f32[256]{0:T(256)} %param.13) | copy-start | bytes 3076
  0.0 1.6 %copy-start.6 = (bf16[4,110592]{1,0:T(4,128)(2,1)S(1)}, bf16[4,110592]{1,0:T(4,128)(2,1)}, u32[]{:S(2)}) copy-start(bf16[4,110592]{1,0:T(4,128)(2,1)} %param.10) | copy-start | bytes 2654212
  1.6 0.7 %copy-start.2 = (s32[2048]{0:T(1024)S(1)}, s32[2048]{0:T(1024)}, u32[]{:S(2)}) copy-start(s32[2048]{0:T(1024)} %param.15) | copy-start | bytes 24580
  1.6 1.0 %copy-start.3 = (bf16[2,400,256]{2,1,0:T(8,128)(2,1)S(1)}, bf16[2,400,256]{2,1,0:T(8,128)(2,1)}, u32[]{:S(2)}) copy-start(bf16[2,400,256]{2,1,0:T(8,128)(2,1)} %constant.86.clone.first) | copy-start | bytes 1228804
  1.6 1.0 %copy-start.4 = (bf16[384,256]{1,0:T(8,128)(2,1)S(1)}, bf16[384,256]{1,0:T(8,128)(2,1)}, u32[]{:S(2)}) copy-start(bf16[384,256]{1,0:T(8,128)(2,1)} %constant.88.clone.third) | copy-start | bytes 589828
  1.6 1.1 %copy-start.5 = (bf16[192,192]{1,0:T(8,128)(2,1)S(1)}, bf16[192,192]{1,0:T(8,128)(2,1)}, u32[]{:S(2)}) copy-start(bf16[192,192]{1,0:T(8,128)(2,1)} %constant.87.clone.second) | copy-start | bytes 221188
  8.7 19.8 %all-to-all-start = ((bf16[16,16,512]{2,1,0:T(8,128)(2,1)}), bf16[16,16,512]{2,1,0:T(8,128)(2,1)S(1)}, u32[]{:S(2)}, u32[]{:S(2)}) async-start(bf16[16,16,512]{2,1,0:T(8,128)(2,1)} %bitcast.3), calls=%async_computation | async-start | bytes 524288 | tf_op jit(solution)/shard_map/all_to_all | solution.py:271
  18.5 0.7 %copy-start.12 = (f32[2]{0:T(128)S(1)}, f32[2]{0:T(128)}, u32[]{:S(2)}) copy-start(f32[2]{0:T(128)} %param.14) | copy-start | bytes 28
  19.2 0.7 %copy-start.11 = (s32[4]{0:T(128)S(1)}, s32[4]{0:T(128)}, u32[]{:S(2)}) copy-start(s32[4]{0:T(128)} %param.16) | copy-start | bytes 52
  19.9 0.7 %copy-start.10 = (f32[4]{0:T(128)S(1)}, f32[4]{0:T(128)}, u32[]{:S(2)}) copy-start(f32[4]{0:T(128)} %param.12) | copy-start | bytes 52
  28.6 5.4 %collective-permute-start = (bf16[128,640]{1,0:T(8,128)(2,1)S(1)}, bf16[128,640]{1,0:T(8,128)(2,1)S(1)}, u32[]{:S(2)}, u32[]{:S(2)}) collective-permute-start(bf16[128,640]{1,0:T(8,128)(2,1)S(1)} %get-tuple-element.16), channel_id=1, source_target_pairs={{0,16},{1,49},{2,18},{3,51},{4,20},{5,53},{6,22},{7,55},{8,24},{9,... | collective-permute-start | bytes 491528 | tf_op jit(solution)/shard_map/ppermute | solution.py:260
  30.3 5.3 %collective-permute-start.1 = (bf16[128,640]{1,0:T(8,128)(2,1)S(1)}, bf16[128,640]{1,0:T(8,128)(2,1)S(1)}, u32[]{:S(2)}, u32[]{:S(2)}) collective-permute-start(bf16[128,640]{1,0:T(8,128)(2,1)S(1)} %get-tuple-element.17), channel_id=1, source_target_pairs={{0,64},{1,193},{2,66},{3,195},{4,68},{5,197},{6,70},{7,199},{8,72}... | collective-permute-start | bytes 491528 | tf_op jit(solution)/shard_map/ppermute | solution.py:260
  31.1 6.2 %collective-permute-start.2 = (bf16[128,640]{1,0:T(8,128)(2,1)S(1)}, bf16[128,640]{1,0:T(8,128)(2,1)S(1)}, u32[]{:S(2)}, u32[]{:S(2)}) collective-permute-start(bf16[128,640]{1,0:T(8,128)(2,1)S(1)} %get-tuple-element.15), channel_id=1, source_target_pairs={{0,80},{1,241},{2,82},{3,243},{4,84},{5,245},{6,86},{7,247},{8,88}... | collective-permute-start | bytes 491528 | tf_op jit(solution)/shard_map/ppermute | solution.py:260
  38.1 0.7 %copy-start.1 = (f32[128,512]{1,0:T(8,128)}, f32[128,512]{1,0:T(8,128)S(1)}, u32[]{:S(2)}) copy-start(f32[128,512]{1,0:T(8,128)S(1)} %get-tuple-element.9.mine) | copy-start | bytes 786436
  38.8 8.3 %collective-permute-start.3 = (bf16[128,512]{1,0:T(8,128)(2,1)S(1)}, bf16[128,512]{1,0:T(8,128)(2,1)S(1)}, u32[]{:S(2)}, u32[]{:S(2)}) collective-permute-start(bf16[128,512]{1,0:T(8,128)(2,1)S(1)} %get-tuple-element.10), channel_id=1, source_target_pairs={{0,240},{1,81},{2,242},{3,83},{4,244},{5,85},{6,246},{7,87},{8,248... | collective-permute-start | bytes 393224 | tf_op jit(solution)/shard_map/ppermute | solution.py:260
  41.7 7.1 %collective-permute-start.4 = (bf16[128,512]{1,0:T(8,128)(2,1)S(1)}, bf16[128,512]{1,0:T(8,128)(2,1)S(1)}, u32[]{:S(2)}, u32[]{:S(2)}) collective-permute-start(bf16[128,512]{1,0:T(8,128)(2,1)S(1)} %get-tuple-element.11), channel_id=1, source_target_pairs={{0,192},{1,65},{2,194},{3,67},{4,196},{5,69},{6,198},{7,71},{8,200... | collective-permute-start | bytes 393224 | tf_op jit(solution)/shard_map/ppermute | solution.py:260
  44.4 6.2 %collective-permute-start.5 = (bf16[128,512]{1,0:T(8,128)(2,1)S(1)}, bf16[128,512]{1,0:T(8,128)(2,1)S(1)}, u32[]{:S(2)}, u32[]{:S(2)}) collective-permute-start(bf16[128,512]{1,0:T(8,128)(2,1)S(1)} %get-tuple-element.12), channel_id=1, source_target_pairs={{0,48},{1,17},{2,50},{3,19},{4,52},{5,21},{6,54},{7,23},{8,56},{9,... | collective-permute-start | bytes 393224 | tf_op jit(solution)/shard_map/ppermute | solution.py:260
  47.1 3.5 %copy-start.7 = (bf16[128,512]{1,0:T(8,128)(2,1)}, bf16[128,512]{1,0:T(8,128)(2,1)S(1)}, u32[]{:S(2)}) copy-start(bf16[128,512]{1,0:T(8,128)(2,1)S(1)} %collective-permute-done.3.first) | copy-start | bytes 393220
  48.8 1.8 %copy-start.8 = (bf16[128,512]{1,0:T(8,128)(2,1)}, bf16[128,512]{1,0:T(8,128)(2,1)S(1)}, u32[]{:S(2)}) copy-start(bf16[128,512]{1,0:T(8,128)(2,1)S(1)} %collective-permute-done.4.second) | copy-start | bytes 393220
  50.6 0.7 %copy-start.9 = (bf16[128,512]{1,0:T(8,128)(2,1)}, bf16[128,512]{1,0:T(8,128)(2,1)S(1)}, u32[]{:S(2)}) copy-start(bf16[128,512]{1,0:T(8,128)(2,1)S(1)} %collective-permute-done.5.third) | copy-start | bytes 393220

commit v3 on v1

--- a/solution.py
+++ b/solution.py
@@ -12,6 +12,7 @@
 BF = jnp.bfloat16
 ZED = ("grow", "zlo", "core")
 ALL = ("bx", "by") + ZED
+CHUNKS = 4
 
 
 def split_table(table):
@@ -72,18 +73,46 @@
     return high, (value - high.astype(jnp.float32)).astype(BF)
 
 
-def density_kernel(cond, val, gvec, first, second, third, out, xh, xl, u, yh, yl, z, dens):
+def density_kernel(
+    cond_far, val_far, gvec_far, first_far, second_far, third_far, out,
+    cond, val, gvec, prod, first, second, third, xh, xl, u, yh, yl, z, dens, sems,
+):
+    wide = xh.shape[1]
+    chunk = GRID // CHUNKS
+    loads = []
+    for n in range(CHUNKS):
+        lanes = pl.ds(wide * chunk * n, wide * chunk)
+        loads.append(
+            [
+                pltpu.make_async_copy(far.at[:, lanes], near.at[:, lanes], sems.at[4 + 2 * n + m])
+                for m, (far, near) in enumerate(((cond_far, cond), (val_far, val)))
+            ]
+        )
+    far_near = ((first_far, first), (second_far, second), (third_far, third), (gvec_far, gvec))
+    copies = [pltpu.make_async_copy(far, near, sems.at[n]) for n, (far, near) in enumerate(far_near)]
+    for copy in sum(loads, []) + copies:
+        copy.start()
     zero = jnp.zeros((32, xh.shape[1]), BF)
-    con = cond[0].astype(jnp.float32)
+    for a in range(GRID):
+        if a % chunk == 0:
+            for load in loads[a // chunk]:
+                load.wait()
+        line = slice(wide * a, wide * a + wide)
+        line = cond[:, line].astype(jnp.float32) * val[:, line].astype(jnp.float32)
+        for tile in range(wide // 128):
+            prod[tile, 4 * a : 4 * a + 4, :] = line[:, 128 * tile : 128 * tile + 128]
     for v in range(4):
         at = 128 * (v // 2) + GRID * (v % 2)
-        high, low = split(con * val[v].astype(jnp.float32))
-        xh[at : at + GRID, :] = high
-        xl[at : at + GRID, :] = low
+        for tile in range(wide // 128):
+            high, low = split(prod[tile, pl.ds(v, GRID, stride=4), :])
+            xh[at : at + GRID, 128 * tile : 128 * tile + 128] = high
+            xl[at : at + GRID, 128 * tile : 128 * tile + 128] = low
     for p in range(2):
         xh[128 * p + 96 : 128 * p + 128, :] = zero
         xl[128 * p + 96 : 128 * p + 128, :] = zero
     n1 = HALF * 8
+    for copy in copies:
+        copy.wait()
     for pair in range(6):
         both = []
         for odd in range(2):
@@ -94,15 +123,17 @@
         high, low = split(jnp.concatenate(both, 1))
         u[:, 16 * pair : 16 * pair + 16, :] = high
         u[:, 96 + 16 * pair : 96 + 16 * pair + 16, :] = low
-    for k in range(HALF):
-        full = dot_nn(second[...], u[k])
-        high, low = split(full[:96] + full[96:])
-        for p in range(2):
-            for s in range(2):
-                rows, lanes = slice(GRID * s, GRID * s + GRID), slice(128 * p, 128 * p + 128)
-                put = (p, slice(GRID * k, GRID * k + GRID), slice(128 * s, 128 * s + 128))
-                yh[put] = high[rows, lanes]
-                yl[put] = low[rows, lanes]
+    for start in range(0, HALF, 5):
+        ks = range(start, start + 5)
+        fulls = [dot_nn(second[...], u[k]) for k in ks]
+        for k, full in zip(ks, fulls):
+            high, low = split(full[:96] + full[96:])
+            for p in range(2):
+                for s in range(2):
+                    rows, lanes = slice(GRID * s, GRID * s + GRID), slice(128 * p, 128 * p + 128)
+                    put = (p, slice(GRID * k, GRID * k + GRID), slice(128 * s, 128 * s + 128))
+                    yh[put] = high[rows, lanes]
+                    yl[put] = low[rows, lanes]
     fill = yh.shape[1] - GRID * HALF
     blank = jnp.zeros((fill, 256), BF)
     for p in range(2):
@@ -148,22 +179,27 @@
             turned.append(tile)
         orders = (jnp.concatenate(tiles, 1), jnp.concatenate(turned, 1))
         for j in range(4):
-            at = 16 * (4 * i + j)
+            at = 16 * (4 * i + 2 * (j % 2) + j // 2)
             both = jnp.concatenate([dens[:, 512 * j : 512 * j + 512], orders[j % 2]], 0)
             out[at : at + 16, :] = both.astype(BF)
 
 
 def density_call(valence, conduction, gvec_index):
     first, second, third = (jnp.asarray(t) for t in tables())
-    cond = jnp.pad(conduction, ((0, 3), (0, 0))).reshape(4, GRID, GRID * GRID)
-    val = valence.reshape(4, GRID, GRID * GRID)
     gvec = gvec_index.reshape(1, -1)
     return pl.pallas_call(
         density_kernel,
         out_shape=jax.ShapeDtypeStruct((256, 512), BF),
-        in_specs=[pl.BlockSpec(memory_space=pltpu.VMEM)] * 6,
+        in_specs=[pl.BlockSpec(memory_space=pl.ANY)] * 6,
         out_specs=pl.BlockSpec(memory_space=pltpu.VMEM),
         scratch_shapes=[
+            pltpu.VMEM(conduction.shape, BF),
+            pltpu.VMEM(valence.shape, BF),
+            pltpu.VMEM(gvec.shape, jnp.int32),
+            pltpu.VMEM((GRID * GRID // 128, 4 * GRID, 128), jnp.float32),
+            pltpu.VMEM(first.shape, BF),
+            pltpu.VMEM(second.shape, BF),
+            pltpu.VMEM(third.shape, BF),
             pltpu.VMEM((256, 2304), BF),
             pltpu.VMEM((256, 2304), BF),
             pltpu.VMEM((HALF, 192, 256), BF),
@@ -171,36 +207,35 @@
             pltpu.VMEM((2, 1280, 256), BF),
             pltpu.VMEM((384, 1280), BF),
             pltpu.VMEM((8, 2048), jnp.float32),
+            pltpu.SemaphoreType.DMA((4 + 2 * CHUNKS,)),
         ],
-        compiler_params=pltpu.CompilerParams(vmem_limit_bytes=48 * 1024 * 1024),
+        compiler_params=pltpu.CompilerParams(vmem_limit_bytes=60 * 1024 * 1024),
         cost_estimate=pl.CostEstimate(flops=5 * 10**9, bytes_accessed=3 * 10**6, transcendentals=0),
         name="density",
-    )(cond, val, gvec, first, second, third)
+    )(conduction, valence, gvec, first, second, third)
 
 
 def product_kernel(turn, weight, own, one, two, three, mine, first, second, third):
-    cols, lefts = [], []
-    for n, block in enumerate((own, one, two, three)):
-        cols.append(block[:, :512])
-        rows = block[:, 512:640].astype(jnp.float32)
-        rows = pltpu.roll(rows, lax.rem(128 - 32 * turn[0], 128), 1)
-        split_rows = rows.reshape(16, 2, 4, 128)
-        swapped = jnp.concatenate([split_rows[:, 1:], -split_rows[:, :1]], 1).reshape(128, 128)
-        parts = []
-        for freq in range(2):
-            scale = weight[n, :, freq : freq + 1]
-            parts.append((scale * rows).astype(BF))
-            parts.append((scale * swapped).astype(BF))
-        lefts.append(jnp.concatenate(parts, 1))
-    left = jnp.concatenate(lefts, 0)
-    right = jnp.concatenate(cols, 0)
+    blocks = (own, one, two, three)
+    twice = []
+    for block in blocks:
+        rows = block[:, 512:640]
+        parts = rows.astype(jnp.float32).reshape(16, 2, 4, 128)
+        swapped = jnp.concatenate([parts[:, 1:], -parts[:, :1]], 1).reshape(128, 128)
+        twice.append(jnp.concatenate([rows, swapped.astype(BF)], 1))
+    lane = lax.broadcasted_iota(jnp.int32, (256, 512), 1)
+    spot = ((lane // 128 + turn[0]) % 4) * 32 + (lane // 4) % 32 + 128 * (lane % 2)
+    copies = jnp.where(lax.broadcasted_iota(jnp.int32, (256, 512), 0) == spot, 1.0, 0.0).astype(BF)
+    spread = dot_nn(jnp.concatenate(twice, 0), copies)
+    scale = weight[...].reshape(512, 2)
+    early = (lax.broadcasted_iota(jnp.int32, (512, 512), 1) // 2) % 2 == 0
+    left = (jnp.where(early, scale[:, 0:1], scale[:, 1:2]) * spread).astype(BF)
+    right = jnp.concatenate([block[:, :512] for block in blocks], 0)
     total = lax.dot_general(left, right, (((0,), (0,)), ((), ())), preferred_element_type=jnp.float32)
-    for part in range(4):
-        at = 128 * part
-        mine[32 * part : 32 * part + 32, :] = total[at : at + 32]
-        first[32 * part : 32 * part + 32, :] = total[at + 32 : at + 64].astype(BF)
-        second[32 * part : 32 * part + 32, :] = total[at + 64 : at + 96].astype(BF)
-        third[32 * part : 32 * part + 32, :] = total[at + 96 : at + 128].astype(BF)
+    mine[...] = total[:128]
+    first[...] = total[128:256].astype(BF)
+    second[...] = total[256:384].astype(BF)
+    third[...] = total[384:].astype(BF)
 
 
 def product_call(turn, weight, blocks):
@@ -238,7 +273,7 @@
     along = lax.axis_size("by")
     group = lax.axis_size("grow") * lax.axis_size("zlo") * lax.axis_size("core")
     sent = sent.reshape(group, 2 * lines, 512)
-    got = lax.all_to_all(sent, ZED, split_axis=0, concat_axis=0, tiled=True)
+    got = lax.all_to_all(sent, ("grow", "core", "zlo"), split_axis=0, concat_axis=0, tiled=True)
     cols = got[:, :lines].reshape(group * lines, 512)
     rows = got[:, lines:].reshape(group * lines, 512)
     x_here = lax.axis_index("bx")
@@ -255,7 +290,8 @@
         blocks[step] = lax.ppermute(block, ALL, pairs) if step else block
     source = lax.rem(place - jnp.arange(across, dtype=jnp.int32) + across, across)
     band = jnp.where(even, source * along + other, other * along + source)
-    bands = (band * group)[:, None] + jnp.arange(group, dtype=jnp.int32)
+    chunk = jnp.arange(group, dtype=jnp.int32)
+    bands = (band * group)[:, None] + chunk // 4 * 4 + chunk % 2 * 2 + chunk % 4 // 2
     energies = jnp.take(cond_energy, bands)
     gap = energies[..., None] - val_energy
     counted = bands[..., None] >= first_band
@@ -267,7 +303,7 @@
     for step in (1, 3, 2):
         pairs = ring_pairs(across, along, group, step, False)
         total = total + lax.ppermute(pieces[step - 1], ALL, pairs).astype(jnp.float32)
-    return jnp.transpose(total.reshape(2, 2, 32, 512), (2, 0, 1, 3)).astype(BF)
+    return total.astype(BF).reshape(32, 2, 2, 512)
 
 
 def solution(mesh):

time: 50.2 us -> 49.1 us (0.978)
  local copies, waits for them, and re-layouts: 6.38 us -> 3.66 us
  Pallas kernels: 6.85 us -> 8.57 us
  waiting for transfers between devices: 18.6 us -> 17.9 us
  starting transfers between devices: 16.8 us -> 17.4 us
    pallas_call x1, Pallas kernels: 6.02 us -> 7.82 us  [density_call(): pl.pallas_call(density_kernel, out_shape=jax.ShapeDtypeStruct((256, 512),...]
    pad x1 -> x0, local copies, waits for them, and re-layouts: 1.55 us -> none  [density_call(): cond = jnp.pad(conduction, ((0, 3), (0, 0))).reshape(4, GRID, GRID * GRID)]
    unnamed x18 -> x8, local copies, waits for them, and re-layouts: 2.82 us -> 1.9 us
    all_to_all x1, waiting for transfers between devices: 7.9 us -> 7.1 us  [on_device(): lax.all_to_all(sent, ('grow', 'core', 'zlo'), split_axis=0, concat_axis=0...]
    convert_element_type x1 -> x0, local copies, waits for them, and re-layouts: 0.79 us -> none  [on_device(): return jnp.transpose(total.reshape(2, 2, 32, 512), (2, 0, 1, 3)).astype(BF)]
    ppermute x3, starting transfers between devices: 2.97 us -> 3.51 us  [on_device(): blocks[step] = lax.ppermute(block, ALL, pairs) if step else block]
    reshape x1, local copies, waits for them, and re-layouts: 0.18 us -> 0.71 us  [on_device(): return total.astype(BF).reshape(32, 2, 2, 512)]
where the time goes in v3:
time: 49.1 us; the launch traced here: 48.5 us
  waiting for transfers between devices  17.9 us (36%)
  starting transfers between devices  17.4 us (35%)
  Pallas kernels  8.57 us (17%)
  local copies, waits for them, and re-layouts  3.66 us (7%)
  other arithmetic  0.8 us (2%)
    all_to_all x1, starting transfers between devices, on_device(): lax.all_to_all(sent, ('grow', 'core', 'zlo'), split_axis=0, concat_axis=0...  8.57 us
    pallas_call x1, Pallas kernels, density_call(): pl.pallas_call(density_kernel, out_shape=jax.ShapeDtypeStruct((256, 512),...  7.82 us
    all_to_all x1, waiting for transfers between devices, on_device(): lax.all_to_all(sent, ('grow', 'core', 'zlo'), split_axis=0, concat_axis=0...  7.1 us
    ppermute x3, waiting for transfers between devices, on_device(): blocks[step] = lax.ppermute(block, ALL, pairs) if step else block  6.35 us
    ppermute x3, starting transfers between devices, on_device(): lax.ppermute(pieces[step - 1], ALL, pairs).astype(jnp.float32)  5.3 us
    ppermute x3, waiting for transfers between devices, on_device(): lax.ppermute(pieces[step - 1], ALL, pairs).astype(jnp.float32)  4.48 us
    ppermute x3, starting transfers between devices, on_device(): blocks[step] = lax.ppermute(block, ALL, pairs) if step else block  3.51 us
    unnamed x8, local copies, waits for them, and re-layouts  1.9 us
  transfers between devices with their start and end apart: 7, of which 7 were waited for; matrix products, arithmetic and copies ran while one was open for 3% of the time, Pallas kernels for 0%

profile of v3, /device:TPU:6, one launch (start us, length us, event | category | flops | bytes accessed | tf_op | source)
XLA Modules:
  0.0 48.5 jit_solution(14853837472315157695)
XLA Ops:
  0.0 0.0 copy-start
  0.0 7.8 %density.1 = bf16[256,512]{1,0:T(8,128)(2,1)} custom-call(bf16[1,110592]{1,0:T(2,128)(2,1)} %cond_far.1, bf16[4,110592]{1,0:T(4,128)(2,1)} %val_far.1, s32[1,2048]{1,0:T(1,128)} %bitcast.12, bf16[2,400,256]{2,1,0:T(8,128)(2,1)} %constant.113.clone.first_far, bf16[192,192]{1,0:T(8,128)(2,1)} %constant.114.clone.second_far, ...), custom_call_target="tpu_custom_call" | custom-call | flops 5000000000 | bytes 3000000 | tf_op jit(solution)/shard_map/density/pallas_call | solution.py:190
  7.8 8.6 %all-to-all-start = ((bf16[16,16,512]{2,1,0:T(8,128)(2,1)}), bf16[16,16,512]{2,1,0:T(8,128)(2,1)S(1)}, u32[]{:S(2)}, u32[]{:S(2)}) async-start(bf16[16,16,512]{2,1,0:T(8,128)(2,1)} %bitcast.11), calls=%async_computation | async-start | bytes 524288 | tf_op jit(solution)/shard_map/all_to_all | solution.py:276
  16.5 0.1 compare_select_fusion
  16.5 0.1 reshape.325
  16.6 0.8 %gather_fusion = f32[64]{0:T(128)S(1)} fusion(f32[256]{0:T(256)S(1)} %copy-done, s32[1024]{0:T(1024)S(1)} %pad_clamp_fusion), kind=kCustom, calls=%fused_computation | custom fusion | bytes 768 | tf_op jit(solution)/shard_map/jit(_take)/gather | solution.py:295
  17.4 0.1 reshape.324
  17.5 0.1 and_select_fusion
  17.6 0.1 add_add_fusion
  17.7 0.7 %copy-done.3 = f32[2]{0:T(128)S(1)} copy-done((f32[2]{0:T(128)S(1)}, f32[2]{0:T(128)}, u32[]{:S(2)}) %copy-start.3) | copy-done | bytes 32
  18.3 0.7 %copy-done.2 = s32[4]{0:T(128)S(1)} copy-done((s32[4]{0:T(128)S(1)}, s32[4]{0:T(128)}, u32[]{:S(2)}) %copy-start.2) | copy-done | bytes 40
  19.0 0.1 broadcast_compare_fusion
  19.1 0.6 %copy-done.1 = f32[4]{0:T(128)S(1)} copy-done((f32[4]{0:T(128)S(1)}, f32[4]{0:T(128)}, u32[]{:S(2)}) %copy-start.1) | copy-done | bytes 40
  19.6 0.1 subtract_multiply_fusion.1
  19.7 7.1 %all-to-all-done = bf16[16,16,512]{2,1,0:T(8,128)(2,1)S(1)} async-done(((bf16[16,16,512]{2,1,0:T(8,128)(2,1)}), bf16[16,16,512]{2,1,0:T(8,128)(2,1)S(1)}, u32[]{:S(2)}, u32[]{:S(2)}) %all-to-all-start) | async-done | bytes 262176 | tf_op jit(solution)/shard_map/all_to_all | solution.py:276
  26.9 0.1 pad_maximum_fusion.3
  27.0 0.9 %collective-permute-start.2 = (bf16[128,640]{1,0:T(8,128)(2,1)S(1)}, bf16[128,640]{1,0:T(8,128)(2,1)S(1)}, u32[]{:S(2)}, u32[]{:S(2)}) collective-permute-start(bf16[128,640]{1,0:T(8,128)(2,1)S(1)} %get-tuple-element.15), channel_id=1, source_target_pairs={{0,192},{1,49},{2,194},{3,51},{4,196},{5,53},{6,198},{7,55},{8,200... | collective-permute-start | bytes 491528 | tf_op jit(solution)/shard_map/ppermute | solution.py:290
  27.9 2.4 %collective-permute-start = (bf16[128,640]{1,0:T(8,128)(2,1)S(1)}, bf16[128,640]{1,0:T(8,128)(2,1)S(1)}, u32[]{:S(2)}, u32[]{:S(2)}) collective-permute-start(bf16[128,640]{1,0:T(8,128)(2,1)S(1)} %get-tuple-element.16), channel_id=1, source_target_pairs={{0,64},{1,17},{2,66},{3,19},{4,68},{5,21},{6,70},{7,23},{8,72},{9,... | collective-permute-start | bytes 491528 | tf_op jit(solution)/shard_map/ppermute | solution.py:290
  30.3 0.2 collective-permute-start.1
  30.5 0.3 select_multiply_fusion
  30.7 2.8 %collective-permute-done.2.three = bf16[128,640]{1,0:T(8,128)(2,1)S(1)} collective-permute-done((bf16[128,640]{1,0:T(8,128)(2,1)S(1)}, bf16[128,640]{1,0:T(8,128)(2,1)S(1)}, u32[]{:S(2)}, u32[]{:S(2)}) %collective-permute-start.2) | collective-permute-done | bytes 163872 | tf_op jit(solution)/shard_map/ppermute | solution.py:290
  33.6 1.3 %collective-permute-done.one = bf16[128,640]{1,0:T(8,128)(2,1)S(1)} collective-permute-done((bf16[128,640]{1,0:T(8,128)(2,1)S(1)}, bf16[128,640]{1,0:T(8,128)(2,1)S(1)}, u32[]{:S(2)}, u32[]{:S(2)}) %collective-permute-start) | collective-permute-done | bytes 163872 | tf_op jit(solution)/shard_map/ppermute | solution.py:290
  34.9 2.2 %collective-permute-done.1.two = bf16[128,640]{1,0:T(8,128)(2,1)S(1)} collective-permute-done((bf16[128,640]{1,0:T(8,128)(2,1)S(1)}, bf16[128,640]{1,0:T(8,128)(2,1)S(1)}, u32[]{:S(2)}, u32[]{:S(2)}) %collective-permute-start.1) | collective-permute-done | bytes 163872 | tf_op jit(solution)/shard_map/ppermute | solution.py:290
  37.1 0.8 %product.1 = (f32[128,512]{1,0:T(8,128)S(1)}, bf16[128,512]{1,0:T(8,128)(2,1)S(1)}, bf16[128,512]{1,0:T(8,128)(2,1)S(1)}, bf16[128,512]{1,0:T(8,128)(2,1)S(1)}) custom-call(s32[1]{0:T(128)} %bitcast.turn, f32[4,128,2]{2,1,0:T(8,128)S(1)} %bitcast.10, bf16[128,640]{1,0:T(8,128)(2,1)S(1)} %get-tuple-element.18.own, ...), custom_call_target="tpu_custom_call" | custom-call | flops 300000000 | bytes 2000000 | tf_op jit(solution)/shard_map/product/pallas_call | solution.py:244
  37.9 1.7 %collective-permute-start.3 = (bf16[128,512]{1,0:T(8,128)(2,1)S(1)}, bf16[128,512]{1,0:T(8,128)(2,1)S(1)}, u32[]{:S(2)}, u32[]{:S(2)}) collective-permute-start(bf16[128,512]{1,0:T(8,128)(2,1)S(1)} %get-tuple-element.10), channel_id=1, source_target_pairs={{0,16},{1,65},{2,18},{3,67},{4,20},{5,69},{6,22},{7,71},{8,24},{9,... | collective-permute-start | bytes 393224 | tf_op jit(solution)/shard_map/ppermute | solution.py:305
  39.5 1.7 %collective-permute-start.4 = (bf16[128,512]{1,0:T(8,128)(2,1)S(1)}, bf16[128,512]{1,0:T(8,128)(2,1)S(1)}, u32[]{:S(2)}, u32[]{:S(2)}) collective-permute-start(bf16[128,512]{1,0:T(8,128)(2,1)S(1)} %get-tuple-element.11), channel_id=1, source_target_pairs={{0,48},{1,193},{2,50},{3,195},{4,52},{5,197},{6,54},{7,199},{8,56}... | collective-permute-start | bytes 393224 | tf_op jit(solution)/shard_map/ppermute | solution.py:305
  41.2 2.0 %collective-permute-start.5 = (bf16[128,512]{1,0:T(8,128)(2,1)S(1)}, bf16[128,512]{1,0:T(8,128)(2,1)S(1)}, u32[]{:S(2)}, u32[]{:S(2)}) collective-permute-start(bf16[128,512]{1,0:T(8,128)(2,1)S(1)} %get-tuple-element.12), channel_id=1, source_target_pairs={{0,32},{1,129},{2,34},{3,131},{4,36},{5,133},{6,38},{7,135},{8,40}... | collective-permute-start | bytes 393224 | tf_op jit(solution)/shard_map/ppermute | solution.py:305
  43.2 1.0 %collective-permute-done.3 = bf16[128,512]{1,0:T(8,128)(2,1)S(1)} collective-permute-done((bf16[128,512]{1,0:T(8,128)(2,1)S(1)}, bf16[128,512]{1,0:T(8,128)(2,1)S(1)}, u32[]{:S(2)}, u32[]{:S(2)}) %collective-permute-start.3) | collective-permute-done | bytes 131104 | tf_op jit(solution)/shard_map/ppermute | solution.py:305
  44.1 0.4 collective-permute-done.4
  44.5 3.2 %collective-permute-done.5 = bf16[128,512]{1,0:T(8,128)(2,1)S(1)} collective-permute-done((bf16[128,512]{1,0:T(8,128)(2,1)S(1)}, bf16[128,512]{1,0:T(8,128)(2,1)S(1)}, u32[]{:S(2)}, u32[]{:S(2)}) %collective-permute-start.5) | collective-permute-done | bytes 131104 | tf_op jit(solution)/shard_map/ppermute | solution.py:305
  47.7 0.1 add_convert_fusion
  47.7 0.7 %reshape.322 = bf16[32,2,2,512]{3,2,1,0:T(2,128)(2,1)} reshape(bf16[128,512]{1,0:T(8,128)(2,1)S(1)} %add_convert_fusion) | data formatting | bytes 262144 | tf_op jit(solution)/shard_map/reshape | solution.py:306
  (12 shorter events, 0.1 us)
Async XLA Ops:
  0.0 16.6 %copy-start = (f32[256]{0:T(256)S(1)}, f32[256]{0:T(256)}, u32[]{:S(2)}) copy-start(f32[256]{0:T(256)} %param.13) | copy-start | bytes 3076
  7.8 19.0 %all-to-all-start = ((bf16[16,16,512]{2,1,0:T(8,128)(2,1)}), bf16[16,16,512]{2,1,0:T(8,128)(2,1)S(1)}, u32[]{:S(2)}, u32[]{:S(2)}) async-start(bf16[16,16,512]{2,1,0:T(8,128)(2,1)} %bitcast.11), calls=%async_computation | async-start | bytes 524288 | tf_op jit(solution)/shard_map/all_to_all | solution.py:276
  17.7 0.7 %copy-start.3 = (f32[2]{0:T(128)S(1)}, f32[2]{0:T(128)}, u32[]{:S(2)}) copy-start(f32[2]{0:T(128)} %param.14) | copy-start | bytes 28
  18.3 0.7 %copy-start.2 = (s32[4]{0:T(128)S(1)}, s32[4]{0:T(128)}, u32[]{:S(2)}) copy-start(s32[4]{0:T(128)} %param.16) | copy-start | bytes 52
  19.0 0.7 %copy-start.1 = (f32[4]{0:T(128)S(1)}, f32[4]{0:T(128)}, u32[]{:S(2)}) copy-start(f32[4]{0:T(128)} %param.12) | copy-start | bytes 52
  27.0 6.6 %collective-permute-start.2 = (bf16[128,640]{1,0:T(8,128)(2,1)S(1)}, bf16[128,640]{1,0:T(8,128)(2,1)S(1)}, u32[]{:S(2)}, u32[]{:S(2)}) collective-permute-start(bf16[128,640]{1,0:T(8,128)(2,1)S(1)} %get-tuple-element.15), channel_id=1, source_target_pairs={{0,192},{1,49},{2,194},{3,51},{4,196},{5,53},{6,198},{7,55},{8,200... | collective-permute-start | bytes 491528 | tf_op jit(solution)/shard_map/ppermute | solution.py:290
  27.9 7.0 %collective-permute-start = (bf16[128,640]{1,0:T(8,128)(2,1)S(1)}, bf16[128,640]{1,0:T(8,128)(2,1)S(1)}, u32[]{:S(2)}, u32[]{:S(2)}) collective-permute-start(bf16[128,640]{1,0:T(8,128)(2,1)S(1)} %get-tuple-element.16), channel_id=1, source_target_pairs={{0,64},{1,17},{2,66},{3,19},{4,68},{5,21},{6,70},{7,23},{8,72},{9,... | collective-permute-start | bytes 491528 | tf_op jit(solution)/shard_map/ppermute | solution.py:290
  30.3 6.8 %collective-permute-start.1 = (bf16[128,640]{1,0:T(8,128)(2,1)S(1)}, bf16[128,640]{1,0:T(8,128)(2,1)S(1)}, u32[]{:S(2)}, u32[]{:S(2)}) collective-permute-start(bf16[128,640]{1,0:T(8,128)(2,1)S(1)} %get-tuple-element.17), channel_id=1, source_target_pairs={{0,128},{1,33},{2,130},{3,35},{4,132},{5,37},{6,134},{7,39},{8,136... | collective-permute-start | bytes 491528 | tf_op jit(solution)/shard_map/ppermute | solution.py:290
  37.9 6.3 %collective-permute-start.3 = (bf16[128,512]{1,0:T(8,128)(2,1)S(1)}, bf16[128,512]{1,0:T(8,128)(2,1)S(1)}, u32[]{:S(2)}, u32[]{:S(2)}) collective-permute-start(bf16[128,512]{1,0:T(8,128)(2,1)S(1)} %get-tuple-element.10), channel_id=1, source_target_pairs={{0,16},{1,65},{2,18},{3,67},{4,20},{5,69},{6,22},{7,71},{8,24},{9,... | collective-permute-start | bytes 393224 | tf_op jit(solution)/shard_map/ppermute | solution.py:305
  39.5 5.0 %collective-permute-start.4 = (bf16[128,512]{1,0:T(8,128)(2,1)S(1)}, bf16[128,512]{1,0:T(8,128)(2,1)S(1)}, u32[]{:S(2)}, u32[]{:S(2)}) collective-permute-start(bf16[128,512]{1,0:T(8,128)(2,1)S(1)} %get-tuple-element.11), channel_id=1, source_target_pairs={{0,48},{1,193},{2,50},{3,195},{4,52},{5,197},{6,54},{7,199},{8,56}... | collective-permute-start | bytes 393224 | tf_op jit(solution)/shard_map/ppermute | solution.py:305
  41.2 6.5 %collective-permute-start.5 = (bf16[128,512]{1,0:T(8,128)(2,1)S(1)}, bf16[128,512]{1,0:T(8,128)(2,1)S(1)}, u32[]{:S(2)}, u32[]{:S(2)}) collective-permute-start(bf16[128,512]{1,0:T(8,128)(2,1)S(1)} %get-tuple-element.12), channel_id=1, source_target_pairs={{0,32},{1,129},{2,34},{3,131},{4,36},{5,133},{6,38},{7,135},{8,40}... | collective-permute-start | bytes 393224 | tf_op jit(solution)/shard_map/ppermute | solution.py:305

commit v4 on v3

--- a/solution.py
+++ b/solution.py
@@ -71,6 +71,23 @@
 def split(value):
     high = value.astype(BF)
     return high, (value - high.astype(jnp.float32)).astype(BF)
+
+
+MEMBERS = (((0, 1), (2, 3)), ((0, 3), (1, 2)))
+
+
+def reduce_order(tiles, quarter, kind):
+    result = []
+    for xs in MEMBERS[kind]:
+        for ys in MEMBERS[kind]:
+            made = None
+            for n in range(4):
+                x, y = xs[n // 2], ys[n % 2]
+                shift = 32 * (n - y) % 128
+                moved = pltpu.roll(tiles[x], shift, 1) if shift else tiles[x]
+                made = moved if made is None else jnp.where(quarter == n, moved, made)
+            result.append(made)
+    return jnp.concatenate(result, 1)
 
 
 def density_kernel(
@@ -169,15 +186,7 @@
     quarter = lax.broadcasted_iota(jnp.int32, (8, 128), 1) // 32
     for i in range(4):
         tiles = [dens[:, 512 * i + 128 * t : 512 * i + 128 * t + 128] for t in range(4)]
-        turned = []
-        for t in range(4):
-            tile = tiles[t]
-            for other in range(4):
-                if other != t:
-                    moved = pltpu.roll(tiles[other], (32 * (other - t)) % 128, 1)
-                    tile = jnp.where(quarter == other, moved, tile)
-            turned.append(tile)
-        orders = (jnp.concatenate(tiles, 1), jnp.concatenate(turned, 1))
+        orders = [reduce_order(tiles, quarter, kind) for kind in (1, 0)]
         for j in range(4):
             at = 16 * (4 * i + 2 * (j % 2) + j // 2)
             both = jnp.concatenate([dens[:, 512 * j : 512 * j + 512], orders[j % 2]], 0)
@@ -224,7 +233,7 @@
         swapped = jnp.concatenate([parts[:, 1:], -parts[:, :1]], 1).reshape(128, 128)
         twice.append(jnp.concatenate([rows, swapped.astype(BF)], 1))
     lane = lax.broadcasted_iota(jnp.int32, (256, 512), 1)
-    spot = ((lane // 128 + turn[0]) % 4) * 32 + (lane // 4) % 32 + 128 * (lane % 2)
+    spot = ((lane // 128) ^ turn[0]) * 32 + (lane // 4) % 32 + 128 * (lane % 2)
     copies = jnp.where(lax.broadcasted_iota(jnp.int32, (256, 512), 0) == spot, 1.0, 0.0).astype(BF)
     spread = dot_nn(jnp.concatenate(twice, 0), copies)
     scale = weight[...].reshape(512, 2)
@@ -252,17 +261,22 @@
     )(turn, weight, *blocks)
 
 
-def ring_pairs(across, along, rest, step, gather):
+def exchange(block, step, gather):
+    across, along = lax.axis_size("bx"), lax.axis_size("by")
+    rest = lax.axis_size("grow") * lax.axis_size("zlo") * lax.axis_size("core")
+
+    def partner(place, kind):
+        return 3 - place if kind else place ^ 1
+
     pairs = []
     for x in range(across):
         for y in range(along):
             for z in range(rest):
-                if (z % 2 == 0) == gather:
-                    to = ((x + step) % across, y)
-                else:
-                    to = (x, (y + step) % along)
-                pairs.append(((x * along + y) * rest + z, (to[0] * along + to[1]) * rest + z))
-    return pairs
+                kind = z % 2 if gather else 1 - z % 2
+                to_x = partner(x, kind) if step // 2 else x
+                to_y = partner(y, kind) if step % 2 else y
+                pairs.append(((x * along + y) * rest + z, (to_x * along + to_y) * rest + z))
+    return lax.ppermute(block, ALL, pairs)
 
 
 def on_device(valence, conduction, val_energy, cond_energy, frequencies, gvec_index, first_band):
@@ -279,17 +293,24 @@
     x_here = lax.axis_index("bx")
     y_here = lax.axis_index("by")
     even = lax.axis_index("core") == 0
-    place = jnp.where(even, x_here, y_here)
-    other = jnp.where(even, y_here, x_here)
+
+    def tile_of(place):
+        return jnp.where(even, (place ^ (place >> 1)) & 1, place >> 1)
+
+    def spot_of(place):
+        return jnp.where(even, place >> 1, place & 1)
+
+    tile = 2 * tile_of(x_here) + tile_of(y_here)
+    spot = 2 * spot_of(x_here) + spot_of(y_here)
     blocks = {}
-    for step in (0, 1, 3, 2):
-        target = lax.rem(place + step, across)
-        part = lax.dynamic_slice_in_dim(rows, target * 128, 128, 1)
+    for step in (0, 3, 2, 1):
+        part = lax.dynamic_slice_in_dim(rows, (tile ^ step) * 128, 128, 1)
         block = jnp.concatenate([cols, part], 1)
-        pairs = ring_pairs(across, along, group, step, True)
-        blocks[step] = lax.ppermute(block, ALL, pairs) if step else block
-    source = lax.rem(place - jnp.arange(across, dtype=jnp.int32) + across, across)
-    band = jnp.where(even, source * along + other, other * along + source)
+        blocks[step] = exchange(block, step, True) if step else block
+    steps = jnp.arange(4, dtype=jnp.int32)
+    x_from = jnp.where(steps // 2 == 0, x_here, jnp.where(even, x_here ^ 1, 3 - x_here))
+    y_from = jnp.where(steps % 2 == 0, y_here, jnp.where(even, y_here ^ 1, 3 - y_here))
+    band = x_from * along + y_from
     chunk = jnp.arange(group, dtype=jnp.int32)
     bands = (band * group)[:, None] + chunk // 4 * 4 + chunk % 2 * 2 + chunk % 4 // 2
     energies = jnp.take(cond_energy, bands)
@@ -299,11 +320,10 @@
     weight = jnp.where(counted[..., None], ratio, 0.0) / (cond_energy.shape[0] * num_val)
     weight = jnp.broadcast_to(weight[:, :, None], (across, group, 2, num_val, frequencies.shape[0]))
     weight = weight.reshape(across, group * lines, frequencies.shape[0])
-    total, *pieces = product_call(other.reshape(1), weight, [blocks[step] for step in range(across)])
-    for step in (1, 3, 2):
-        pairs = ring_pairs(across, along, group, step, False)
-        total = total + lax.ppermute(pieces[step - 1], ALL, pairs).astype(jnp.float32)
-    return total.astype(BF).reshape(32, 2, 2, 512)
+    total, *pieces = product_call(spot.reshape(1), weight, [blocks[step] for step in range(4)])
+    for step in (3, 2, 1):
+        total = total + exchange(pieces[step - 1], step, False).astype(jnp.float32)
+    return total.astype(BF).reshape(32, frequencies.shape[0], 2, 512)
 
 
 def solution(mesh):

time: 49.1 us -> 48.8 us (level)
  starting transfers between devices: 17.4 us -> 18.1 us
  waiting for transfers between devices: 17.9 us -> 17.3 us
    ppermute x6, starting transfers between devices: 8.81 us -> 9.57 us  [exchange(): return lax.ppermute(block, ALL, pairs)]
    ppermute x6, waiting for transfers between devices: 10.8 us -> 10.2 us  [exchange(): return lax.ppermute(block, ALL, pairs)]
where the time goes in v4:
time: 48.8 us; the launch traced here: 48.5 us
  starting transfers between devices  18.1 us (37%)
  waiting for transfers between devices  17.3 us (35%)
  Pallas kernels  8.54 us (18%)
  local copies, waits for them, and re-layouts  3.66 us (8%)
  other arithmetic  0.8 us (2%)
    ppermute x6, waiting for transfers between devices, exchange(): return lax.ppermute(block, ALL, pairs)  10.2 us
    ppermute x6, starting transfers between devices, exchange(): return lax.ppermute(block, ALL, pairs)  9.57 us
    all_to_all x1, starting transfers between devices, on_device(): lax.all_to_all(sent, ('grow', 'core', 'zlo'), split_axis=0, concat_axis=0...  8.57 us
    pallas_call x1, Pallas kernels, density_call(): pl.pallas_call(density_kernel, out_shape=jax.ShapeDtypeStruct((256, 512),...  7.82 us
    all_to_all x1, waiting for transfers between devices, on_device(): lax.all_to_all(sent, ('grow', 'core', 'zlo'), split_axis=0, concat_axis=0...  7.1 us
    unnamed x8, local copies, waits for them, and re-layouts  1.9 us
  transfers between devices with their start and end apart: 7, of which 7 were waited for; matrix products, arithmetic and copies ran while one was open for 3% of the time, Pallas kernels for 0%

profile of v4, /device:TPU:6, one launch (start us, length us, event | category | flops | bytes accessed | tf_op | source)
XLA Modules:
  0.0 48.5 jit_solution(6286534582309354517)
XLA Ops:
  0.0 0.0 copy-start
  0.0 7.8 %density.1 = bf16[256,512]{1,0:T(8,128)(2,1)} custom-call(bf16[1,110592]{1,0:T(2,128)(2,1)} %cond_far.1, bf16[4,110592]{1,0:T(4,128)(2,1)} %val_far.1, s32[1,2048]{1,0:T(1,128)} %bitcast.12, bf16[2,400,256]{2,1,0:T(8,128)(2,1)} %constant.124.clone.first_far, bf16[192,192]{1,0:T(8,128)(2,1)} %constant.125.clone.second_far, ...), custom_call_target="tpu_custom_call" | custom-call | flops 5000000000 | bytes 3000000 | tf_op jit(solution)/shard_map/density/pallas_call | solution.py:199
  7.8 8.6 %all-to-all-start = ((bf16[16,16,512]{2,1,0:T(8,128)(2,1)}), bf16[16,16,512]{2,1,0:T(8,128)(2,1)S(1)}, u32[]{:S(2)}, u32[]{:S(2)}) async-start(bf16[16,16,512]{2,1,0:T(8,128)(2,1)} %bitcast.11), calls=%async_computation | async-start | bytes 524288 | tf_op jit(solution)/shard_map/all_to_all | solution.py:290
  16.5 0.1 compare_select_fusion
  16.6 0.1 reshape.336
  16.6 0.8 %gather_fusion = f32[64]{0:T(128)S(1)} fusion(f32[256]{0:T(256)S(1)} %copy-done, s32[1024]{0:T(1024)S(1)} %pad_clamp_fusion), kind=kCustom, calls=%fused_computation | custom fusion | bytes 768 | tf_op jit(solution)/shard_map/jit(_take)/gather | solution.py:316
  17.4 0.1 reshape.335
  17.5 0.1 and_select_fusion
  17.6 0.1 add_add_fusion
  17.7 0.7 %copy-done.3 = f32[2]{0:T(128)S(1)} copy-done((f32[2]{0:T(128)S(1)}, f32[2]{0:T(128)}, u32[]{:S(2)}) %copy-start.3) | copy-done | bytes 32
  18.3 0.7 %copy-done.2 = s32[4]{0:T(128)S(1)} copy-done((s32[4]{0:T(128)S(1)}, s32[4]{0:T(128)}, u32[]{:S(2)}) %copy-start.2) | copy-done | bytes 40
  19.0 0.1 broadcast_compare_fusion
  19.1 0.6 %copy-done.1 = f32[4]{0:T(128)S(1)} copy-done((f32[4]{0:T(128)S(1)}, f32[4]{0:T(128)}, u32[]{:S(2)}) %copy-start.1) | copy-done | bytes 40
  19.6 0.1 subtract_multiply_fusion.1
  19.7 7.1 %all-to-all-done = bf16[16,16,512]{2,1,0:T(8,128)(2,1)S(1)} async-done(((bf16[16,16,512]{2,1,0:T(8,128)(2,1)}), bf16[16,16,512]{2,1,0:T(8,128)(2,1)S(1)}, u32[]{:S(2)}, u32[]{:S(2)}) %all-to-all-start) | async-done | bytes 262176 | tf_op jit(solution)/shard_map/all_to_all | solution.py:290
  26.9 0.1 pad_maximum_fusion.3
  27.0 1.9 %collective-permute-start.2 = (bf16[128,640]{1,0:T(8,128)(2,1)S(1)}, bf16[128,640]{1,0:T(8,128)(2,1)S(1)}, u32[]{:S(2)}, u32[]{:S(2)}) collective-permute-start(bf16[128,640]{1,0:T(8,128)(2,1)S(1)} %get-tuple-element.15), channel_id=1, source_target_pairs={{0,80},{1,241},{2,82},{3,243},{4,84},{5,245},{6,86},{7,247},{8,88}... | collective-permute-start | bytes 491528 | tf_op jit(solution)/shard_map/ppermute | solution.py:279
  28.9 0.4 collective-permute-start
  29.3 1.2 %collective-permute-start.1 = (bf16[128,640]{1,0:T(8,128)(2,1)S(1)}, bf16[128,640]{1,0:T(8,128)(2,1)S(1)}, u32[]{:S(2)}, u32[]{:S(2)}) collective-permute-start(bf16[128,640]{1,0:T(8,128)(2,1)S(1)} %get-tuple-element.17), channel_id=1, source_target_pairs={{0,64},{1,193},{2,66},{3,195},{4,68},{5,197},{6,70},{7,199},{8,72}... | collective-permute-start | bytes 491528 | tf_op jit(solution)/shard_map/ppermute | solution.py:279
  30.5 0.3 select_multiply_fusion
  30.8 2.5 %collective-permute-done.2.three = bf16[128,640]{1,0:T(8,128)(2,1)S(1)} collective-permute-done((bf16[128,640]{1,0:T(8,128)(2,1)S(1)}, bf16[128,640]{1,0:T(8,128)(2,1)S(1)}, u32[]{:S(2)}, u32[]{:S(2)}) %collective-permute-start.2) | collective-permute-done | bytes 163872 | tf_op jit(solution)/shard_map/ppermute | solution.py:279
  33.3 1.7 %collective-permute-done.one = bf16[128,640]{1,0:T(8,128)(2,1)S(1)} collective-permute-done((bf16[128,640]{1,0:T(8,128)(2,1)S(1)}, bf16[128,640]{1,0:T(8,128)(2,1)S(1)}, u32[]{:S(2)}, u32[]{:S(2)}) %collective-permute-start) | collective-permute-done | bytes 163872 | tf_op jit(solution)/shard_map/ppermute | solution.py:279
  35.0 0.2 collective-permute-done.1.two
  35.2 0.7 %product.1 = (f32[128,512]{1,0:T(8,128)S(1)}, bf16[128,512]{1,0:T(8,128)(2,1)S(1)}, bf16[128,512]{1,0:T(8,128)(2,1)S(1)}, bf16[128,512]{1,0:T(8,128)(2,1)S(1)}) custom-call(s32[1]{0:T(128)} %bitcast.turn, f32[4,128,2]{2,1,0:T(8,128)S(1)} %bitcast.10, bf16[128,640]{1,0:T(8,128)(2,1)S(1)} %get-tuple-element.18.own, ...), custom_call_target="tpu_custom_call" | custom-call | flops 300000000 | bytes 2000000 | tf_op jit(solution)/shard_map/product/pallas_call | solution.py:253
  36.0 3.1 %collective-permute-start.3 = (bf16[128,512]{1,0:T(8,128)(2,1)S(1)}, bf16[128,512]{1,0:T(8,128)(2,1)S(1)}, u32[]{:S(2)}, u32[]{:S(2)}) collective-permute-start(bf16[128,512]{1,0:T(8,128)(2,1)S(1)} %get-tuple-element.10), channel_id=1, source_target_pairs={{0,240},{1,81},{2,242},{3,83},{4,244},{5,85},{6,246},{7,87},{8,248... | collective-permute-start | bytes 393224 | tf_op jit(solution)/shard_map/ppermute | solution.py:279
  39.1 2.5 %collective-permute-start.4 = (bf16[128,512]{1,0:T(8,128)(2,1)S(1)}, bf16[128,512]{1,0:T(8,128)(2,1)S(1)}, u32[]{:S(2)}, u32[]{:S(2)}) collective-permute-start(bf16[128,512]{1,0:T(8,128)(2,1)S(1)} %get-tuple-element.11), channel_id=1, source_target_pairs={{0,192},{1,65},{2,194},{3,67},{4,196},{5,69},{6,198},{7,71},{8,200... | collective-permute-start | bytes 393224 | tf_op jit(solution)/shard_map/ppermute | solution.py:279
  41.6 0.4 collective-permute-start.5
  41.9 2.4 %collective-permute-done.3 = bf16[128,512]{1,0:T(8,128)(2,1)S(1)} collective-permute-done((bf16[128,512]{1,0:T(8,128)(2,1)S(1)}, bf16[128,512]{1,0:T(8,128)(2,1)S(1)}, u32[]{:S(2)}, u32[]{:S(2)}) %collective-permute-start.3) | collective-permute-done | bytes 131104 | tf_op jit(solution)/shard_map/ppermute | solution.py:279
  44.3 1.6 %collective-permute-done.4 = bf16[128,512]{1,0:T(8,128)(2,1)S(1)} collective-permute-done((bf16[128,512]{1,0:T(8,128)(2,1)S(1)}, bf16[128,512]{1,0:T(8,128)(2,1)S(1)}, u32[]{:S(2)}, u32[]{:S(2)}) %collective-permute-start.4) | collective-permute-done | bytes 131104 | tf_op jit(solution)/shard_map/ppermute | solution.py:279
  45.9 1.8 %collective-permute-done.5 = bf16[128,512]{1,0:T(8,128)(2,1)S(1)} collective-permute-done((bf16[128,512]{1,0:T(8,128)(2,1)S(1)}, bf16[128,512]{1,0:T(8,128)(2,1)S(1)}, u32[]{:S(2)}, u32[]{:S(2)}) %collective-permute-start.5) | collective-permute-done | bytes 131104 | tf_op jit(solution)/shard_map/ppermute | solution.py:279
  47.7 0.1 add_convert_fusion
  47.8 0.7 %reshape.333 = bf16[32,2,2,512]{3,2,1,0:T(2,128)(2,1)} reshape(bf16[128,512]{1,0:T(8,128)(2,1)S(1)} %add_convert_fusion) | data formatting | bytes 262144 | tf_op jit(solution)/shard_map/reshape | solution.py:326
  (12 shorter events, 0.1 us)
Async XLA Ops:
  0.0 16.6 %copy-start = (f32[256]{0:T(256)S(1)}, f32[256]{0:T(256)}, u32[]{:S(2)}) copy-start(f32[256]{0:T(256)} %param.13) | copy-start | bytes 3076
  7.8 19.0 %all-to-all-start = ((bf16[16,16,512]{2,1,0:T(8,128)(2,1)}), bf16[16,16,512]{2,1,0:T(8,128)(2,1)S(1)}, u32[]{:S(2)}, u32[]{:S(2)}) async-start(bf16[16,16,512]{2,1,0:T(8,128)(2,1)} %bitcast.11), calls=%async_computation | async-start | bytes 524288 | tf_op jit(solution)/shard_map/all_to_all | solution.py:290
  17.7 0.7 %copy-start.3 = (f32[2]{0:T(128)S(1)}, f32[2]{0:T(128)}, u32[]{:S(2)}) copy-start(f32[2]{0:T(128)} %param.14) | copy-start | bytes 28
  18.3 0.7 %copy-start.2 = (s32[4]{0:T(128)S(1)}, s32[4]{0:T(128)}, u32[]{:S(2)}) copy-start(s32[4]{0:T(128)} %param.16) | copy-start | bytes 52
  19.0 0.7 %copy-start.1 = (f32[4]{0:T(128)S(1)}, f32[4]{0:T(128)}, u32[]{:S(2)}) copy-start(f32[4]{0:T(128)} %param.12) | copy-start | bytes 52
  27.0 6.4 %collective-permute-start.2 = (bf16[128,640]{1,0:T(8,128)(2,1)S(1)}, bf16[128,640]{1,0:T(8,128)(2,1)S(1)}, u32[]{:S(2)}, u32[]{:S(2)}) collective-permute-start(bf16[128,640]{1,0:T(8,128)(2,1)S(1)} %get-tuple-element.15), channel_id=1, source_target_pairs={{0,80},{1,241},{2,82},{3,243},{4,84},{5,245},{6,86},{7,247},{8,88}... | collective-permute-start | bytes 491528 | tf_op jit(solution)/shard_map/ppermute | solution.py:279
  28.9 6.1 %collective-permute-start = (bf16[128,640]{1,0:T(8,128)(2,1)S(1)}, bf16[128,640]{1,0:T(8,128)(2,1)S(1)}, u32[]{:S(2)}, u32[]{:S(2)}) collective-permute-start(bf16[128,640]{1,0:T(8,128)(2,1)S(1)} %get-tuple-element.16), channel_id=1, source_target_pairs={{0,16},{1,49},{2,18},{3,51},{4,20},{5,53},{6,22},{7,55},{8,24},{9,... | collective-permute-start | bytes 491528 | tf_op jit(solution)/shard_map/ppermute | solution.py:279
  29.3 5.8 %collective-permute-start.1 = (bf16[128,640]{1,0:T(8,128)(2,1)S(1)}, bf16[128,640]{1,0:T(8,128)(2,1)S(1)}, u32[]{:S(2)}, u32[]{:S(2)}) collective-permute-start(bf16[128,640]{1,0:T(8,128)(2,1)S(1)} %get-tuple-element.17), channel_id=1, source_target_pairs={{0,64},{1,193},{2,66},{3,195},{4,68},{5,197},{6,70},{7,199},{8,72}... | collective-permute-start | bytes 491528 | tf_op jit(solution)/shard_map/ppermute | solution.py:279
  36.0 8.4 %collective-permute-start.3 = (bf16[128,512]{1,0:T(8,128)(2,1)S(1)}, bf16[128,512]{1,0:T(8,128)(2,1)S(1)}, u32[]{:S(2)}, u32[]{:S(2)}) collective-permute-start(bf16[128,512]{1,0:T(8,128)(2,1)S(1)} %get-tuple-element.10), channel_id=1, source_target_pairs={{0,240},{1,81},{2,242},{3,83},{4,244},{5,85},{6,246},{7,87},{8,248... | collective-permute-start | bytes 393224 | tf_op jit(solution)/shard_map/ppermute | solution.py:279
  39.1 6.8 %collective-permute-start.4 = (bf16[128,512]{1,0:T(8,128)(2,1)S(1)}, bf16[128,512]{1,0:T(8,128)(2,1)S(1)}, u32[]{:S(2)}, u32[]{:S(2)}) collective-permute-start(bf16[128,512]{1,0:T(8,128)(2,1)S(1)} %get-tuple-element.11), channel_id=1, source_target_pairs={{0,192},{1,65},{2,194},{3,67},{4,196},{5,69},{6,198},{7,71},{8,200... | collective-permute-start | bytes 393224 | tf_op jit(solution)/shard_map/ppermute | solution.py:279
  41.6 6.2 %collective-permute-start.5 = (bf16[128,512]{1,0:T(8,128)(2,1)S(1)}, bf16[128,512]{1,0:T(8,128)(2,1)S(1)}, u32[]{:S(2)}, u32[]{:S(2)}) collective-permute-start(bf16[128,512]{1,0:T(8,128)(2,1)S(1)} %get-tuple-element.12), channel_id=1, source_target_pairs={{0,48},{1,17},{2,50},{3,19},{4,52},{5,21},{6,54},{7,23},{8,56},{9,... | collective-permute-start | bytes 393224 | tf_op jit(solution)/shard_map/ppermute | solution.py:279

commit v5 on v4

--- a/solution.py
+++ b/solution.py
@@ -186,7 +186,7 @@
     quarter = lax.broadcasted_iota(jnp.int32, (8, 128), 1) // 32
     for i in range(4):
         tiles = [dens[:, 512 * i + 128 * t : 512 * i + 128 * t + 128] for t in range(4)]
-        orders = [reduce_order(tiles, quarter, kind) for kind in (1, 0)]
+        orders = [reduce_order(tiles, quarter, kind) for kind in (0, 1)]
         for j in range(4):
             at = 16 * (4 * i + 2 * (j % 2) + j // 2)
             both = jnp.concatenate([dens[:, 512 * j : 512 * j + 512], orders[j % 2]], 0)
@@ -272,7 +272,7 @@
     for x in range(across):
         for y in range(along):
             for z in range(rest):
-                kind = z % 2 if gather else 1 - z % 2
+                kind = 1 - z % 2 if gather else z % 2
                 to_x = partner(x, kind) if step // 2 else x
                 to_y = partner(y, kind) if step % 2 else y
                 pairs.append(((x * along + y) * rest + z, (to_x * along + to_y) * rest + z))
@@ -292,7 +292,7 @@
     rows = got[:, lines:].reshape(group * lines, 512)
     x_here = lax.axis_index("bx")
     y_here = lax.axis_index("by")
-    even = lax.axis_index("core") == 0
+    even = lax.axis_index("core") == 1
 
     def tile_of(place):
         return jnp.where(even, (place ^ (place >> 1)) & 1, place >> 1)

time: 48.8 us -> 48.8 us (level)
  the two profiles are of different devices: /device:TPU:6 before, /device:TPU:16 now
where the time goes in v5:
time: 48.8 us; the launch traced here: 48.6 us
  waiting for transfers between devices  17.8 us (36%)
  starting transfers between devices  17.6 us (36%)
  Pallas kernels  8.55 us (18%)
  local copies, waits for them, and re-layouts  3.66 us (8%)
  other arithmetic  0.8 us (2%)
    ppermute x6, waiting for transfers between devices, exchange(): return lax.ppermute(block, ALL, pairs)  10.7 us
    ppermute x6, starting transfers between devices, exchange(): return lax.ppermute(block, ALL, pairs)  9.03 us
    all_to_all x1, starting transfers between devices, on_device(): lax.all_to_all(sent, ('grow', 'core', 'zlo'), split_axis=0, concat_axis=0...  8.58 us
    pallas_call x1, Pallas kernels, density_call(): pl.pallas_call(density_kernel, out_shape=jax.ShapeDtypeStruct((256, 512),...  7.82 us
    all_to_all x1, waiting for transfers between devices, on_device(): lax.all_to_all(sent, ('grow', 'core', 'zlo'), split_axis=0, concat_axis=0...  7.1 us
    unnamed x8, local copies, waits for them, and re-layouts  1.9 us
  transfers between devices with their start and end apart: 7, of which 7 were waited for; matrix products, arithmetic and copies ran while one was open for 3% of the time, Pallas kernels for 0%

profile of v5, /device:TPU:16, one launch (start us, length us, event | category | flops | bytes accessed | tf_op | source)
XLA Modules:
  0.0 48.6 jit_solution(783915903887273607)
XLA Ops:
  0.0 0.0 copy-start
  0.0 7.8 %density.1 = bf16[256,512]{1,0:T(8,128)(2,1)} custom-call(bf16[1,110592]{1,0:T(2,128)(2,1)} %cond_far.1, bf16[4,110592]{1,0:T(4,128)(2,1)} %val_far.1, s32[1,2048]{1,0:T(1,128)} %bitcast.12, bf16[2,400,256]{2,1,0:T(8,128)(2,1)} %constant.124.clone.first_far, bf16[192,192]{1,0:T(8,128)(2,1)} %constant.125.clone.second_far, ...), custom_call_target="tpu_custom_call" | custom-call | flops 5000000000 | bytes 3000000 | tf_op jit(solution)/shard_map/density/pallas_call | solution.py:199
  7.8 8.6 %all-to-all-start = ((bf16[16,16,512]{2,1,0:T(8,128)(2,1)}), bf16[16,16,512]{2,1,0:T(8,128)(2,1)S(1)}, u32[]{:S(2)}, u32[]{:S(2)}) async-start(bf16[16,16,512]{2,1,0:T(8,128)(2,1)} %bitcast.11), calls=%async_computation | async-start | bytes 524288 | tf_op jit(solution)/shard_map/all_to_all | solution.py:290
  16.5 0.1 compare_select_fusion
  16.6 0.1 reshape.336
  16.7 0.8 %gather_fusion = f32[64]{0:T(128)S(1)} fusion(f32[256]{0:T(256)S(1)} %copy-done, s32[1024]{0:T(1024)S(1)} %pad_clamp_fusion), kind=kCustom, calls=%fused_computation | custom fusion | bytes 768 | tf_op jit(solution)/shard_map/jit(_take)/gather | solution.py:316
  17.4 0.1 reshape.335
  17.5 0.1 and_select_fusion
  17.6 0.1 add_add_fusion
  17.7 0.7 %copy-done.3 = f32[2]{0:T(128)S(1)} copy-done((f32[2]{0:T(128)S(1)}, f32[2]{0:T(128)}, u32[]{:S(2)}) %copy-start.3) | copy-done | bytes 32
  18.3 0.7 %copy-done.2 = s32[4]{0:T(128)S(1)} copy-done((s32[4]{0:T(128)S(1)}, s32[4]{0:T(128)}, u32[]{:S(2)}) %copy-start.2) | copy-done | bytes 40
  19.0 0.1 broadcast_compare_fusion
  19.1 0.6 %copy-done.1 = f32[4]{0:T(128)S(1)} copy-done((f32[4]{0:T(128)S(1)}, f32[4]{0:T(128)}, u32[]{:S(2)}) %copy-start.1) | copy-done | bytes 40
  19.7 0.1 subtract_multiply_fusion.1
  19.7 7.1 %all-to-all-done = bf16[16,16,512]{2,1,0:T(8,128)(2,1)S(1)} async-done(((bf16[16,16,512]{2,1,0:T(8,128)(2,1)}), bf16[16,16,512]{2,1,0:T(8,128)(2,1)S(1)}, u32[]{:S(2)}, u32[]{:S(2)}) %all-to-all-start) | async-done | bytes 262176 | tf_op jit(solution)/shard_map/all_to_all | solution.py:290
  26.9 0.1 pad_maximum_fusion.3
  27.0 2.7 %collective-permute-start.2 = (bf16[128,640]{1,0:T(8,128)(2,1)S(1)}, bf16[128,640]{1,0:T(8,128)(2,1)S(1)}, u32[]{:S(2)}, u32[]{:S(2)}) collective-permute-start(bf16[128,640]{1,0:T(8,128)(2,1)S(1)} %get-tuple-element.15), channel_id=1, source_target_pairs={{0,240},{1,81},{2,242},{3,83},{4,244},{5,85},{6,246},{7,87},{8,248... | collective-permute-start | bytes 491528 | tf_op jit(solution)/shard_map/ppermute | solution.py:279
  29.7 1.6 %collective-permute-start = (bf16[128,640]{1,0:T(8,128)(2,1)S(1)}, bf16[128,640]{1,0:T(8,128)(2,1)S(1)}, u32[]{:S(2)}, u32[]{:S(2)}) collective-permute-start(bf16[128,640]{1,0:T(8,128)(2,1)S(1)} %get-tuple-element.16), channel_id=1, source_target_pairs={{0,48},{1,17},{2,50},{3,19},{4,52},{5,21},{6,54},{7,23},{8,56},{9,... | collective-permute-start | bytes 491528 | tf_op jit(solution)/shard_map/ppermute | solution.py:279
  31.3 0.5 collective-permute-start.1
  31.7 0.3 select_multiply_fusion
  32.0 2.6 %collective-permute-done.2.three = bf16[128,640]{1,0:T(8,128)(2,1)S(1)} collective-permute-done((bf16[128,640]{1,0:T(8,128)(2,1)S(1)}, bf16[128,640]{1,0:T(8,128)(2,1)S(1)}, u32[]{:S(2)}, u32[]{:S(2)}) %collective-permute-start.2) | collective-permute-done | bytes 163872 | tf_op jit(solution)/shard_map/ppermute | solution.py:279
  34.6 1.7 %collective-permute-done.one = bf16[128,640]{1,0:T(8,128)(2,1)S(1)} collective-permute-done((bf16[128,640]{1,0:T(8,128)(2,1)S(1)}, bf16[128,640]{1,0:T(8,128)(2,1)S(1)}, u32[]{:S(2)}, u32[]{:S(2)}) %collective-permute-start) | collective-permute-done | bytes 163872 | tf_op jit(solution)/shard_map/ppermute | solution.py:279
  36.2 1.6 %collective-permute-done.1.two = bf16[128,640]{1,0:T(8,128)(2,1)S(1)} collective-permute-done((bf16[128,640]{1,0:T(8,128)(2,1)S(1)}, bf16[128,640]{1,0:T(8,128)(2,1)S(1)}, u32[]{:S(2)}, u32[]{:S(2)}) %collective-permute-start.1) | collective-permute-done | bytes 163872 | tf_op jit(solution)/shard_map/ppermute | solution.py:279
  37.8 0.7 %product.1 = (f32[128,512]{1,0:T(8,128)S(1)}, bf16[128,512]{1,0:T(8,128)(2,1)S(1)}, bf16[128,512]{1,0:T(8,128)(2,1)S(1)}, bf16[128,512]{1,0:T(8,128)(2,1)S(1)}) custom-call(s32[1]{0:T(128)} %bitcast.turn, f32[4,128,2]{2,1,0:T(8,128)S(1)} %bitcast.10, bf16[128,640]{1,0:T(8,128)(2,1)S(1)} %get-tuple-element.18.own, ...), custom_call_target="tpu_custom_call" | custom-call | flops 300000000 | bytes 2000000 | tf_op jit(solution)/shard_map/product/pallas_call | solution.py:253
  38.6 1.0 %collective-permute-start.3 = (bf16[128,512]{1,0:T(8,128)(2,1)S(1)}, bf16[128,512]{1,0:T(8,128)(2,1)S(1)}, u32[]{:S(2)}, u32[]{:S(2)}) collective-permute-start(bf16[128,512]{1,0:T(8,128)(2,1)S(1)} %get-tuple-element.10), channel_id=1, source_target_pairs={{0,80},{1,241},{2,82},{3,243},{4,84},{5,245},{6,86},{7,247},{8,88}... | collective-permute-start | bytes 393224 | tf_op jit(solution)/shard_map/ppermute | solution.py:279
  39.6 3.2 %collective-permute-start.4 = (bf16[128,512]{1,0:T(8,128)(2,1)S(1)}, bf16[128,512]{1,0:T(8,128)(2,1)S(1)}, u32[]{:S(2)}, u32[]{:S(2)}) collective-permute-start(bf16[128,512]{1,0:T(8,128)(2,1)S(1)} %get-tuple-element.11), channel_id=1, source_target_pairs={{0,64},{1,193},{2,66},{3,195},{4,68},{5,197},{6,70},{7,199},{8,72}... | collective-permute-start | bytes 393224 | tf_op jit(solution)/shard_map/ppermute | solution.py:279
  42.8 0.0 collective-permute-start.5
  42.8 1.7 %collective-permute-done.3 = bf16[128,512]{1,0:T(8,128)(2,1)S(1)} collective-permute-done((bf16[128,512]{1,0:T(8,128)(2,1)S(1)}, bf16[128,512]{1,0:T(8,128)(2,1)S(1)}, u32[]{:S(2)}, u32[]{:S(2)}) %collective-permute-start.3) | collective-permute-done | bytes 131104 | tf_op jit(solution)/shard_map/ppermute | solution.py:279
  44.5 2.6 %collective-permute-done.4 = bf16[128,512]{1,0:T(8,128)(2,1)S(1)} collective-permute-done((bf16[128,512]{1,0:T(8,128)(2,1)S(1)}, bf16[128,512]{1,0:T(8,128)(2,1)S(1)}, u32[]{:S(2)}, u32[]{:S(2)}) %collective-permute-start.4) | collective-permute-done | bytes 131104 | tf_op jit(solution)/shard_map/ppermute | solution.py:279
  47.2 0.6 %collective-permute-done.5 = bf16[128,512]{1,0:T(8,128)(2,1)S(1)} collective-permute-done((bf16[128,512]{1,0:T(8,128)(2,1)S(1)}, bf16[128,512]{1,0:T(8,128)(2,1)S(1)}, u32[]{:S(2)}, u32[]{:S(2)}) %collective-permute-start.5) | collective-permute-done | bytes 131104 | tf_op jit(solution)/shard_map/ppermute | solution.py:279
  47.8 0.1 add_convert_fusion
  47.9 0.7 %reshape.333 = bf16[32,2,2,512]{3,2,1,0:T(2,128)(2,1)} reshape(bf16[128,512]{1,0:T(8,128)(2,1)S(1)} %add_convert_fusion) | data formatting | bytes 262144 | tf_op jit(solution)/shard_map/reshape | solution.py:326
  (12 shorter events, 0.1 us)
Async XLA Ops:
  0.0 16.7 %copy-start = (f32[256]{0:T(256)S(1)}, f32[256]{0:T(256)}, u32[]{:S(2)}) copy-start(f32[256]{0:T(256)} %param.13) | copy-start | bytes 3076
  7.8 19.0 %all-to-all-start = ((bf16[16,16,512]{2,1,0:T(8,128)(2,1)}), bf16[16,16,512]{2,1,0:T(8,128)(2,1)S(1)}, u32[]{:S(2)}, u32[]{:S(2)}) async-start(bf16[16,16,512]{2,1,0:T(8,128)(2,1)} %bitcast.11), calls=%async_computation | async-start | bytes 524288 | tf_op jit(solution)/shard_map/all_to_all | solution.py:290
  17.7 0.7 %copy-start.3 = (f32[2]{0:T(128)S(1)}, f32[2]{0:T(128)}, u32[]{:S(2)}) copy-start(f32[2]{0:T(128)} %param.14) | copy-start | bytes 28
  18.3 0.7 %copy-start.2 = (s32[4]{0:T(128)S(1)}, s32[4]{0:T(128)}, u32[]{:S(2)}) copy-start(s32[4]{0:T(128)} %param.16) | copy-start | bytes 52
  19.0 0.7 %copy-start.1 = (f32[4]{0:T(128)S(1)}, f32[4]{0:T(128)}, u32[]{:S(2)}) copy-start(f32[4]{0:T(128)} %param.12) | copy-start | bytes 52
  27.0 7.6 %collective-permute-start.2 = (bf16[128,640]{1,0:T(8,128)(2,1)S(1)}, bf16[128,640]{1,0:T(8,128)(2,1)S(1)}, u32[]{:S(2)}, u32[]{:S(2)}) collective-permute-start(bf16[128,640]{1,0:T(8,128)(2,1)S(1)} %get-tuple-element.15), channel_id=1, source_target_pairs={{0,240},{1,81},{2,242},{3,83},{4,244},{5,85},{6,246},{7,87},{8,248... | collective-permute-start | bytes 491528 | tf_op jit(solution)/shard_map/ppermute | solution.py:279
  29.7 6.5 %collective-permute-start = (bf16[128,640]{1,0:T(8,128)(2,1)S(1)}, bf16[128,640]{1,0:T(8,128)(2,1)S(1)}, u32[]{:S(2)}, u32[]{:S(2)}) collective-permute-start(bf16[128,640]{1,0:T(8,128)(2,1)S(1)} %get-tuple-element.16), channel_id=1, source_target_pairs={{0,48},{1,17},{2,50},{3,19},{4,52},{5,21},{6,54},{7,23},{8,56},{9,... | collective-permute-start | bytes 491528 | tf_op jit(solution)/shard_map/ppermute | solution.py:279
  31.3 6.5 %collective-permute-start.1 = (bf16[128,640]{1,0:T(8,128)(2,1)S(1)}, bf16[128,640]{1,0:T(8,128)(2,1)S(1)}, u32[]{:S(2)}, u32[]{:S(2)}) collective-permute-start(bf16[128,640]{1,0:T(8,128)(2,1)S(1)} %get-tuple-element.17), channel_id=1, source_target_pairs={{0,192},{1,65},{2,194},{3,67},{4,196},{5,69},{6,198},{7,71},{8,200... | collective-permute-start | bytes 491528 | tf_op jit(solution)/shard_map/ppermute | solution.py:279
  38.6 6.0 %collective-permute-start.3 = (bf16[128,512]{1,0:T(8,128)(2,1)S(1)}, bf16[128,512]{1,0:T(8,128)(2,1)S(1)}, u32[]{:S(2)}, u32[]{:S(2)}) collective-permute-start(bf16[128,512]{1,0:T(8,128)(2,1)S(1)} %get-tuple-element.10), channel_id=1, source_target_pairs={{0,80},{1,241},{2,82},{3,243},{4,84},{5,245},{6,86},{7,247},{8,88}... | collective-permute-start | bytes 393224 | tf_op jit(solution)/shard_map/ppermute | solution.py:279
  39.6 7.6 %collective-permute-start.4 = (bf16[128,512]{1,0:T(8,128)(2,1)S(1)}, bf16[128,512]{1,0:T(8,128)(2,1)S(1)}, u32[]{:S(2)}, u32[]{:S(2)}) collective-permute-start(bf16[128,512]{1,0:T(8,128)(2,1)S(1)} %get-tuple-element.11), channel_id=1, source_target_pairs={{0,64},{1,193},{2,66},{3,195},{4,68},{5,197},{6,70},{7,199},{8,72}... | collective-permute-start | bytes 393224 | tf_op jit(solution)/shard_map/ppermute | solution.py:279
  42.8 5.0 %collective-permute-start.5 = (bf16[128,512]{1,0:T(8,128)(2,1)S(1)}, bf16[128,512]{1,0:T(8,128)(2,1)S(1)}, u32[]{:S(2)}, u32[]{:S(2)}) collective-permute-start(bf16[128,512]{1,0:T(8,128)(2,1)S(1)} %get-tuple-element.12), channel_id=1, source_target_pairs={{0,16},{1,49},{2,18},{3,51},{4,20},{5,53},{6,22},{7,55},{8,24},{9,... | collective-permute-start | bytes 393224 | tf_op jit(solution)/shard_map/ppermute | solution.py:279

commit v6 on v4

--- a/solution.py
+++ b/solution.py
@@ -188,7 +188,7 @@
         tiles = [dens[:, 512 * i + 128 * t : 512 * i + 128 * t + 128] for t in range(4)]
         orders = [reduce_order(tiles, quarter, kind) for kind in (1, 0)]
         for j in range(4):
-            at = 16 * (4 * i + 2 * (j % 2) + j // 2)
+            at = 16 * (8 * (j // 2) + 4 * (j % 2) + i)
             both = jnp.concatenate([dens[:, 512 * j : 512 * j + 512], orders[j % 2]], 0)
             out[at : at + 16, :] = both.astype(BF)
 
@@ -287,7 +287,7 @@
     along = lax.axis_size("by")
     group = lax.axis_size("grow") * lax.axis_size("zlo") * lax.axis_size("core")
     sent = sent.reshape(group, 2 * lines, 512)
-    got = lax.all_to_all(sent, ("grow", "core", "zlo"), split_axis=0, concat_axis=0, tiled=True)
+    got = lax.all_to_all(sent, ("zlo", "core", "grow"), split_axis=0, concat_axis=0, tiled=True)
     cols = got[:, :lines].reshape(group * lines, 512)
     rows = got[:, lines:].reshape(group * lines, 512)
     x_here = lax.axis_index("bx")
@@ -312,7 +312,7 @@
     y_from = jnp.where(steps % 2 == 0, y_here, jnp.where(even, y_here ^ 1, 3 - y_here))
     band = x_from * along + y_from
     chunk = jnp.arange(group, dtype=jnp.int32)
-    bands = (band * group)[:, None] + chunk // 4 * 4 + chunk % 2 * 2 + chunk % 4 // 2
+    bands = (band * group)[:, None] + chunk % 4 * 4 + chunk // 8 * 2 + chunk // 4 % 2
     energies = jnp.take(cond_energy, bands)
     gap = energies[..., None] - val_energy
     counted = bands[..., None] >= first_band

time: 48.8 us -> 48.4 us (level)
  no operation moved by 1% of the time
where the time goes in v6:
time: 48.4 us; the launch traced here: 48.1 us
  starting transfers between devices  18.1 us (37%)
  waiting for transfers between devices  16.9 us (35%)
  Pallas kernels  8.54 us (18%)
  local copies, waits for them, and re-layouts  3.66 us (8%)
  other arithmetic  0.79 us (2%)
    ppermute x6, waiting for transfers between devices, exchange(): return lax.ppermute(block, ALL, pairs)  10.2 us
    ppermute x6, starting transfers between devices, exchange(): return lax.ppermute(block, ALL, pairs)  9.57 us
    all_to_all x1, starting transfers between devices, on_device(): lax.all_to_all(sent, ('zlo', 'core', 'grow'), split_axis=0, concat_axis=0...  8.57 us
    pallas_call x1, Pallas kernels, density_call(): pl.pallas_call(density_kernel, out_shape=jax.ShapeDtypeStruct((256, 512),...  7.82 us
    all_to_all x1, waiting for transfers between devices, on_device(): lax.all_to_all(sent, ('zlo', 'core', 'grow'), split_axis=0, concat_axis=0...  6.7 us
    unnamed x8, local copies, waits for them, and re-layouts  1.9 us
  transfers between devices with their start and end apart: 7, of which 7 were waited for; matrix products, arithmetic and copies ran while one was open for 3% of the time, Pallas kernels for 0%

profile of v6, /device:TPU:6, one launch (start us, length us, event | category | flops | bytes accessed | tf_op | source)
XLA Modules:
  0.0 48.1 jit_solution(10522258513415034206)
XLA Ops:
  0.0 0.0 copy-start
  0.0 7.8 %density.1 = bf16[256,512]{1,0:T(8,128)(2,1)} custom-call(bf16[1,110592]{1,0:T(2,128)(2,1)} %cond_far.1, bf16[4,110592]{1,0:T(4,128)(2,1)} %val_far.1, s32[1,2048]{1,0:T(1,128)} %bitcast.12, bf16[2,400,256]{2,1,0:T(8,128)(2,1)} %constant.128.clone.first_far, bf16[192,192]{1,0:T(8,128)(2,1)} %constant.129.clone.second_far, ...), custom_call_target="tpu_custom_call" | custom-call | flops 5000000000 | bytes 3000000 | tf_op jit(solution)/shard_map/density/pallas_call | solution.py:199
  7.8 8.6 %all-to-all-start = ((bf16[16,16,512]{2,1,0:T(8,128)(2,1)}), bf16[16,16,512]{2,1,0:T(8,128)(2,1)S(1)}, u32[]{:S(2)}, u32[]{:S(2)}) async-start(bf16[16,16,512]{2,1,0:T(8,128)(2,1)} %bitcast.11), calls=%async_computation | async-start | bytes 524288 | tf_op jit(solution)/shard_map/all_to_all | solution.py:290
  16.5 0.1 compare_select_fusion
  16.5 0.1 reshape.334
  16.6 0.8 %gather_fusion = f32[64]{0:T(128)S(1)} fusion(f32[256]{0:T(256)S(1)} %copy-done, s32[1024]{0:T(1024)S(1)} %pad_clamp_fusion), kind=kCustom, calls=%fused_computation | custom fusion | bytes 768 | tf_op jit(solution)/shard_map/jit(_take)/gather | solution.py:316
  17.4 0.1 reshape.333
  17.5 0.1 and_select_fusion
  17.6 0.1 add_add_fusion
  17.7 0.7 %copy-done.3 = f32[2]{0:T(128)S(1)} copy-done((f32[2]{0:T(128)S(1)}, f32[2]{0:T(128)}, u32[]{:S(2)}) %copy-start.3) | copy-done | bytes 32
  18.3 0.7 %copy-done.2 = s32[4]{0:T(128)S(1)} copy-done((s32[4]{0:T(128)S(1)}, s32[4]{0:T(128)}, u32[]{:S(2)}) %copy-start.2) | copy-done | bytes 40
  19.0 0.1 broadcast_compare_fusion
  19.1 0.6 %copy-done.1 = f32[4]{0:T(128)S(1)} copy-done((f32[4]{0:T(128)S(1)}, f32[4]{0:T(128)}, u32[]{:S(2)}) %copy-start.1) | copy-done | bytes 40
  19.6 0.1 subtract_multiply_fusion.1
  19.7 6.7 %all-to-all-done = bf16[16,16,512]{2,1,0:T(8,128)(2,1)S(1)} async-done(((bf16[16,16,512]{2,1,0:T(8,128)(2,1)}), bf16[16,16,512]{2,1,0:T(8,128)(2,1)S(1)}, u32[]{:S(2)}, u32[]{:S(2)}) %all-to-all-start) | async-done | bytes 262176 | tf_op jit(solution)/shard_map/all_to_all | solution.py:290
  26.5 0.1 pad_maximum_fusion.3
  26.6 1.9 %collective-permute-start.2 = (bf16[128,640]{1,0:T(8,128)(2,1)S(1)}, bf16[128,640]{1,0:T(8,128)(2,1)S(1)}, u32[]{:S(2)}, u32[]{:S(2)}) collective-permute-start(bf16[128,640]{1,0:T(8,128)(2,1)S(1)} %get-tuple-element.15), channel_id=1, source_target_pairs={{0,80},{1,241},{2,82},{3,243},{4,84},{5,245},{6,86},{7,247},{8,88}... | collective-permute-start | bytes 491528 | tf_op jit(solution)/shard_map/ppermute | solution.py:279
  28.5 0.4 collective-permute-start
  28.9 1.2 %collective-permute-start.1 = (bf16[128,640]{1,0:T(8,128)(2,1)S(1)}, bf16[128,640]{1,0:T(8,128)(2,1)S(1)}, u32[]{:S(2)}, u32[]{:S(2)}) collective-permute-start(bf16[128,640]{1,0:T(8,128)(2,1)S(1)} %get-tuple-element.17), channel_id=1, source_target_pairs={{0,64},{1,193},{2,66},{3,195},{4,68},{5,197},{6,70},{7,199},{8,72}... | collective-permute-start | bytes 491528 | tf_op jit(solution)/shard_map/ppermute | solution.py:279
  30.1 0.3 select_multiply_fusion
  30.4 2.5 %collective-permute-done.2.three = bf16[128,640]{1,0:T(8,128)(2,1)S(1)} collective-permute-done((bf16[128,640]{1,0:T(8,128)(2,1)S(1)}, bf16[128,640]{1,0:T(8,128)(2,1)S(1)}, u32[]{:S(2)}, u32[]{:S(2)}) %collective-permute-start.2) | collective-permute-done | bytes 163872 | tf_op jit(solution)/shard_map/ppermute | solution.py:279
  32.9 1.7 %collective-permute-done.one = bf16[128,640]{1,0:T(8,128)(2,1)S(1)} collective-permute-done((bf16[128,640]{1,0:T(8,128)(2,1)S(1)}, bf16[128,640]{1,0:T(8,128)(2,1)S(1)}, u32[]{:S(2)}, u32[]{:S(2)}) %collective-permute-start) | collective-permute-done | bytes 163872 | tf_op jit(solution)/shard_map/ppermute | solution.py:279
  34.6 0.2 collective-permute-done.1.two
  34.8 0.7 %product.1 = (f32[128,512]{1,0:T(8,128)S(1)}, bf16[128,512]{1,0:T(8,128)(2,1)S(1)}, bf16[128,512]{1,0:T(8,128)(2,1)S(1)}, bf16[128,512]{1,0:T(8,128)(2,1)S(1)}) custom-call(s32[1]{0:T(128)} %bitcast.turn, f32[4,128,2]{2,1,0:T(8,128)S(1)} %bitcast.10, bf16[128,640]{1,0:T(8,128)(2,1)S(1)} %get-tuple-element.18.own, ...), custom_call_target="tpu_custom_call" | custom-call | flops 300000000 | bytes 2000000 | tf_op jit(solution)/shard_map/product/pallas_call | solution.py:253
  35.6 3.2 %collective-permute-start.3 = (bf16[128,512]{1,0:T(8,128)(2,1)S(1)}, bf16[128,512]{1,0:T(8,128)(2,1)S(1)}, u32[]{:S(2)}, u32[]{:S(2)}) collective-permute-start(bf16[128,512]{1,0:T(8,128)(2,1)S(1)} %get-tuple-element.10), channel_id=1, source_target_pairs={{0,240},{1,81},{2,242},{3,83},{4,244},{5,85},{6,246},{7,87},{8,248... | collective-permute-start | bytes 393224 | tf_op jit(solution)/shard_map/ppermute | solution.py:279
  38.7 2.5 %collective-permute-start.4 = (bf16[128,512]{1,0:T(8,128)(2,1)S(1)}, bf16[128,512]{1,0:T(8,128)(2,1)S(1)}, u32[]{:S(2)}, u32[]{:S(2)}) collective-permute-start(bf16[128,512]{1,0:T(8,128)(2,1)S(1)} %get-tuple-element.11), channel_id=1, source_target_pairs={{0,192},{1,65},{2,194},{3,67},{4,196},{5,69},{6,198},{7,71},{8,200... | collective-permute-start | bytes 393224 | tf_op jit(solution)/shard_map/ppermute | solution.py:279
  41.2 0.4 collective-permute-start.5
  41.5 2.4 %collective-permute-done.3 = bf16[128,512]{1,0:T(8,128)(2,1)S(1)} collective-permute-done((bf16[128,512]{1,0:T(8,128)(2,1)S(1)}, bf16[128,512]{1,0:T(8,128)(2,1)S(1)}, u32[]{:S(2)}, u32[]{:S(2)}) %collective-permute-start.3) | collective-permute-done | bytes 131104 | tf_op jit(solution)/shard_map/ppermute | solution.py:279
  43.9 1.6 %collective-permute-done.4 = bf16[128,512]{1,0:T(8,128)(2,1)S(1)} collective-permute-done((bf16[128,512]{1,0:T(8,128)(2,1)S(1)}, bf16[128,512]{1,0:T(8,128)(2,1)S(1)}, u32[]{:S(2)}, u32[]{:S(2)}) %collective-permute-start.4) | collective-permute-done | bytes 131104 | tf_op jit(solution)/shard_map/ppermute | solution.py:279
  45.5 1.8 %collective-permute-done.5 = bf16[128,512]{1,0:T(8,128)(2,1)S(1)} collective-permute-done((bf16[128,512]{1,0:T(8,128)(2,1)S(1)}, bf16[128,512]{1,0:T(8,128)(2,1)S(1)}, u32[]{:S(2)}, u32[]{:S(2)}) %collective-permute-start.5) | collective-permute-done | bytes 131104 | tf_op jit(solution)/shard_map/ppermute | solution.py:279
  47.3 0.1 add_convert_fusion
  47.4 0.7 %reshape.331 = bf16[32,2,2,512]{3,2,1,0:T(2,128)(2,1)} reshape(bf16[128,512]{1,0:T(8,128)(2,1)S(1)} %add_convert_fusion) | data formatting | bytes 262144 | tf_op jit(solution)/shard_map/reshape | solution.py:326
  (12 shorter events, 0.1 us)
Async XLA Ops:
  0.0 16.6 %copy-start = (f32[256]{0:T(256)S(1)}, f32[256]{0:T(256)}, u32[]{:S(2)}) copy-start(f32[256]{0:T(256)} %param.13) | copy-start | bytes 3076
  7.8 18.6 %all-to-all-start = ((bf16[16,16,512]{2,1,0:T(8,128)(2,1)}), bf16[16,16,512]{2,1,0:T(8,128)(2,1)S(1)}, u32[]{:S(2)}, u32[]{:S(2)}) async-start(bf16[16,16,512]{2,1,0:T(8,128)(2,1)} %bitcast.11), calls=%async_computation | async-start | bytes 524288 | tf_op jit(solution)/shard_map/all_to_all | solution.py:290
  17.7 0.7 %copy-start.3 = (f32[2]{0:T(128)S(1)}, f32[2]{0:T(128)}, u32[]{:S(2)}) copy-start(f32[2]{0:T(128)} %param.14) | copy-start | bytes 28
  18.3 0.7 %copy-start.2 = (s32[4]{0:T(128)S(1)}, s32[4]{0:T(128)}, u32[]{:S(2)}) copy-start(s32[4]{0:T(128)} %param.16) | copy-start | bytes 52
  19.0 0.7 %copy-start.1 = (f32[4]{0:T(128)S(1)}, f32[4]{0:T(128)}, u32[]{:S(2)}) copy-start(f32[4]{0:T(128)} %param.12) | copy-start | bytes 52
  26.6 6.4 %collective-permute-start.2 = (bf16[128,640]{1,0:T(8,128)(2,1)S(1)}, bf16[128,640]{1,0:T(8,128)(2,1)S(1)}, u32[]{:S(2)}, u32[]{:S(2)}) collective-permute-start(bf16[128,640]{1,0:T(8,128)(2,1)S(1)} %get-tuple-element.15), channel_id=1, source_target_pairs={{0,80},{1,241},{2,82},{3,243},{4,84},{5,245},{6,86},{7,247},{8,88}... | collective-permute-start | bytes 491528 | tf_op jit(solution)/shard_map/ppermute | solution.py:279
  28.5 6.1 %collective-permute-start = (bf16[128,640]{1,0:T(8,128)(2,1)S(1)}, bf16[128,640]{1,0:T(8,128)(2,1)S(1)}, u32[]{:S(2)}, u32[]{:S(2)}) collective-permute-start(bf16[128,640]{1,0:T(8,128)(2,1)S(1)} %get-tuple-element.16), channel_id=1, source_target_pairs={{0,16},{1,49},{2,18},{3,51},{4,20},{5,53},{6,22},{7,55},{8,24},{9,... | collective-permute-start | bytes 491528 | tf_op jit(solution)/shard_map/ppermute | solution.py:279
  28.9 5.8 %collective-permute-start.1 = (bf16[128,640]{1,0:T(8,128)(2,1)S(1)}, bf16[128,640]{1,0:T(8,128)(2,1)S(1)}, u32[]{:S(2)}, u32[]{:S(2)}) collective-permute-start(bf16[128,640]{1,0:T(8,128)(2,1)S(1)} %get-tuple-element.17), channel_id=1, source_target_pairs={{0,64},{1,193},{2,66},{3,195},{4,68},{5,197},{6,70},{7,199},{8,72}... | collective-permute-start | bytes 491528 | tf_op jit(solution)/shard_map/ppermute | solution.py:279
  35.6 8.4 %collective-permute-start.3 = (bf16[128,512]{1,0:T(8,128)(2,1)S(1)}, bf16[128,512]{1,0:T(8,128)(2,1)S(1)}, u32[]{:S(2)}, u32[]{:S(2)}) collective-permute-start(bf16[128,512]{1,0:T(8,128)(2,1)S(1)} %get-tuple-element.10), channel_id=1, source_target_pairs={{0,240},{1,81},{2,242},{3,83},{4,244},{5,85},{6,246},{7,87},{8,248... | collective-permute-start | bytes 393224 | tf_op jit(solution)/shard_map/ppermute | solution.py:279
  38.7 6.8 %collective-permute-start.4 = (bf16[128,512]{1,0:T(8,128)(2,1)S(1)}, bf16[128,512]{1,0:T(8,128)(2,1)S(1)}, u32[]{:S(2)}, u32[]{:S(2)}) collective-permute-start(bf16[128,512]{1,0:T(8,128)(2,1)S(1)} %get-tuple-element.11), channel_id=1, source_target_pairs={{0,192},{1,65},{2,194},{3,67},{4,196},{5,69},{6,198},{7,71},{8,200... | collective-permute-start | bytes 393224 | tf_op jit(solution)/shard_map/ppermute | solution.py:279
  41.2 6.2 %collective-permute-start.5 = (bf16[128,512]{1,0:T(8,128)(2,1)S(1)}, bf16[128,512]{1,0:T(8,128)(2,1)S(1)}, u32[]{:S(2)}, u32[]{:S(2)}) collective-permute-start(bf16[128,512]{1,0:T(8,128)(2,1)S(1)} %get-tuple-element.12), channel_id=1, source_target_pairs={{0,48},{1,17},{2,50},{3,19},{4,52},{5,21},{6,54},{7,23},{8,56},{9,... | collective-permute-start | bytes 393224 | tf_op jit(solution)/shard_map/ppermute | solution.py:279

commit v7 on v6

--- a/solution.py
+++ b/solution.py
@@ -142,9 +142,9 @@
         u[:, 96 + 16 * pair : 96 + 16 * pair + 16, :] = low
     for start in range(0, HALF, 5):
         ks = range(start, start + 5)
-        fulls = [dot_nn(second[...], u[k]) for k in ks]
+        fulls = [dot_nn(second[:96], u[k]) + dot_nn(second[96:, :96], u[k, :96]) for k in ks]
         for k, full in zip(ks, fulls):
-            high, low = split(full[:96] + full[96:])
+            high, low = split(full)
             for p in range(2):
                 for s in range(2):
                     rows, lanes = slice(GRID * s, GRID * s + GRID), slice(128 * p, 128 * p + 128)

time: 48.4 us -> 48.4 us (level)
  no operation moved by 1% of the time
where the time goes in v7:
time: 48.4 us; the launch traced here: 48.1 us
  starting transfers between devices  18.2 us (38%)
  waiting for transfers between devices  16.9 us (35%)
  Pallas kernels  8.55 us (18%)
  local copies, waits for them, and re-layouts  3.66 us (8%)
  other arithmetic  0.79 us (2%)
    ppermute x6, waiting for transfers between devices, exchange(): return lax.ppermute(block, ALL, pairs)  10.2 us
    ppermute x6, starting transfers between devices, exchange(): return lax.ppermute(block, ALL, pairs)  9.57 us
    all_to_all x1, starting transfers between devices, on_device(): lax.all_to_all(sent, ('zlo', 'core', 'grow'), split_axis=0, concat_axis=0...  8.58 us
    pallas_call x1, Pallas kernels, density_call(): pl.pallas_call(density_kernel, out_shape=jax.ShapeDtypeStruct((256, 512),...  7.83 us
    all_to_all x1, waiting for transfers between devices, on_device(): lax.all_to_all(sent, ('zlo', 'core', 'grow'), split_axis=0, concat_axis=0...  6.7 us
    unnamed x8, local copies, waits for them, and re-layouts  1.9 us
  transfers between devices with their start and end apart: 7, of which 7 were waited for; matrix products, arithmetic and copies ran while one was open for 3% of the time, Pallas kernels for 0%

profile of v7, /device:TPU:6, one launch (start us, length us, event | category | flops | bytes accessed | tf_op | source)
XLA Modules:
  0.0 48.1 jit_solution(6320242941792427430)
XLA Ops:
  0.0 0.0 copy-start
  0.0 7.8 %density.1 = bf16[256,512]{1,0:T(8,128)(2,1)} custom-call(bf16[1,110592]{1,0:T(2,128)(2,1)} %cond_far.1, bf16[4,110592]{1,0:T(4,128)(2,1)} %val_far.1, s32[1,2048]{1,0:T(1,128)} %bitcast.12, bf16[2,400,256]{2,1,0:T(8,128)(2,1)} %constant.128.clone.first_far, bf16[192,192]{1,0:T(8,128)(2,1)} %constant.129.clone.second_far, ...), custom_call_target="tpu_custom_call" | custom-call | flops 5000000000 | bytes 3000000 | tf_op jit(solution)/shard_map/density/pallas_call | solution.py:199
  7.8 8.6 %all-to-all-start = ((bf16[16,16,512]{2,1,0:T(8,128)(2,1)}), bf16[16,16,512]{2,1,0:T(8,128)(2,1)S(1)}, u32[]{:S(2)}, u32[]{:S(2)}) async-start(bf16[16,16,512]{2,1,0:T(8,128)(2,1)} %bitcast.11), calls=%async_computation | async-start | bytes 524288 | tf_op jit(solution)/shard_map/all_to_all | solution.py:290
  16.5 0.1 compare_select_fusion
  16.6 0.1 reshape.334
  16.7 0.8 %gather_fusion = f32[64]{0:T(128)S(1)} fusion(f32[256]{0:T(256)S(1)} %copy-done, s32[1024]{0:T(1024)S(1)} %pad_clamp_fusion), kind=kCustom, calls=%fused_computation | custom fusion | bytes 768 | tf_op jit(solution)/shard_map/jit(_take)/gather | solution.py:316
  17.5 0.1 reshape.333
  17.5 0.1 and_select_fusion
  17.6 0.1 add_add_fusion
  17.7 0.7 %copy-done.3 = f32[2]{0:T(128)S(1)} copy-done((f32[2]{0:T(128)S(1)}, f32[2]{0:T(128)}, u32[]{:S(2)}) %copy-start.3) | copy-done | bytes 32
  18.4 0.7 %copy-done.2 = s32[4]{0:T(128)S(1)} copy-done((s32[4]{0:T(128)S(1)}, s32[4]{0:T(128)}, u32[]{:S(2)}) %copy-start.2) | copy-done | bytes 40
  19.0 0.1 broadcast_compare_fusion
  19.1 0.6 %copy-done.1 = f32[4]{0:T(128)S(1)} copy-done((f32[4]{0:T(128)S(1)}, f32[4]{0:T(128)}, u32[]{:S(2)}) %copy-start.1) | copy-done | bytes 40
  19.7 0.1 subtract_multiply_fusion.1
  19.7 6.7 %all-to-all-done = bf16[16,16,512]{2,1,0:T(8,128)(2,1)S(1)} async-done(((bf16[16,16,512]{2,1,0:T(8,128)(2,1)}), bf16[16,16,512]{2,1,0:T(8,128)(2,1)S(1)}, u32[]{:S(2)}, u32[]{:S(2)}) %all-to-all-start) | async-done | bytes 262176 | tf_op jit(solution)/shard_map/all_to_all | solution.py:290
  26.5 0.1 pad_maximum_fusion.3
  26.6 1.9 %collective-permute-start.2 = (bf16[128,640]{1,0:T(8,128)(2,1)S(1)}, bf16[128,640]{1,0:T(8,128)(2,1)S(1)}, u32[]{:S(2)}, u32[]{:S(2)}) collective-permute-start(bf16[128,640]{1,0:T(8,128)(2,1)S(1)} %get-tuple-element.15), channel_id=1, source_target_pairs={{0,80},{1,241},{2,82},{3,243},{4,84},{5,245},{6,86},{7,247},{8,88}... | collective-permute-start | bytes 491528 | tf_op jit(solution)/shard_map/ppermute | solution.py:279
  28.5 0.4 collective-permute-start
  28.9 1.2 %collective-permute-start.1 = (bf16[128,640]{1,0:T(8,128)(2,1)S(1)}, bf16[128,640]{1,0:T(8,128)(2,1)S(1)}, u32[]{:S(2)}, u32[]{:S(2)}) collective-permute-start(bf16[128,640]{1,0:T(8,128)(2,1)S(1)} %get-tuple-element.17), channel_id=1, source_target_pairs={{0,64},{1,193},{2,66},{3,195},{4,68},{5,197},{6,70},{7,199},{8,72}... | collective-permute-start | bytes 491528 | tf_op jit(solution)/shard_map/ppermute | solution.py:279
  30.1 0.3 select_multiply_fusion
  30.4 2.5 %collective-permute-done.2.three = bf16[128,640]{1,0:T(8,128)(2,1)S(1)} collective-permute-done((bf16[128,640]{1,0:T(8,128)(2,1)S(1)}, bf16[128,640]{1,0:T(8,128)(2,1)S(1)}, u32[]{:S(2)}, u32[]{:S(2)}) %collective-permute-start.2) | collective-permute-done | bytes 163872 | tf_op jit(solution)/shard_map/ppermute | solution.py:279
  33.0 1.7 %collective-permute-done.one = bf16[128,640]{1,0:T(8,128)(2,1)S(1)} collective-permute-done((bf16[128,640]{1,0:T(8,128)(2,1)S(1)}, bf16[128,640]{1,0:T(8,128)(2,1)S(1)}, u32[]{:S(2)}, u32[]{:S(2)}) %collective-permute-start) | collective-permute-done | bytes 163872 | tf_op jit(solution)/shard_map/ppermute | solution.py:279
  34.6 0.2 collective-permute-done.1.two
  34.8 0.7 %product.1 = (f32[128,512]{1,0:T(8,128)S(1)}, bf16[128,512]{1,0:T(8,128)(2,1)S(1)}, bf16[128,512]{1,0:T(8,128)(2,1)S(1)}, bf16[128,512]{1,0:T(8,128)(2,1)S(1)}) custom-call(s32[1]{0:T(128)} %bitcast.turn, f32[4,128,2]{2,1,0:T(8,128)S(1)} %bitcast.10, bf16[128,640]{1,0:T(8,128)(2,1)S(1)} %get-tuple-element.18.own, ...), custom_call_target="tpu_custom_call" | custom-call | flops 300000000 | bytes 2000000 | tf_op jit(solution)/shard_map/product/pallas_call | solution.py:253
  35.6 3.1 %collective-permute-start.3 = (bf16[128,512]{1,0:T(8,128)(2,1)S(1)}, bf16[128,512]{1,0:T(8,128)(2,1)S(1)}, u32[]{:S(2)}, u32[]{:S(2)}) collective-permute-start(bf16[128,512]{1,0:T(8,128)(2,1)S(1)} %get-tuple-element.10), channel_id=1, source_target_pairs={{0,240},{1,81},{2,242},{3,83},{4,244},{5,85},{6,246},{7,87},{8,248... | collective-permute-start | bytes 393224 | tf_op jit(solution)/shard_map/ppermute | solution.py:279
  38.7 2.5 %collective-permute-start.4 = (bf16[128,512]{1,0:T(8,128)(2,1)S(1)}, bf16[128,512]{1,0:T(8,128)(2,1)S(1)}, u32[]{:S(2)}, u32[]{:S(2)}) collective-permute-start(bf16[128,512]{1,0:T(8,128)(2,1)S(1)} %get-tuple-element.11), channel_id=1, source_target_pairs={{0,192},{1,65},{2,194},{3,67},{4,196},{5,69},{6,198},{7,71},{8,200... | collective-permute-start | bytes 393224 | tf_op jit(solution)/shard_map/ppermute | solution.py:279
  41.2 0.4 collective-permute-start.5
  41.6 2.4 %collective-permute-done.3 = bf16[128,512]{1,0:T(8,128)(2,1)S(1)} collective-permute-done((bf16[128,512]{1,0:T(8,128)(2,1)S(1)}, bf16[128,512]{1,0:T(8,128)(2,1)S(1)}, u32[]{:S(2)}, u32[]{:S(2)}) %collective-permute-start.3) | collective-permute-done | bytes 131104 | tf_op jit(solution)/shard_map/ppermute | solution.py:279
  43.9 1.6 %collective-permute-done.4 = bf16[128,512]{1,0:T(8,128)(2,1)S(1)} collective-permute-done((bf16[128,512]{1,0:T(8,128)(2,1)S(1)}, bf16[128,512]{1,0:T(8,128)(2,1)S(1)}, u32[]{:S(2)}, u32[]{:S(2)}) %collective-permute-start.4) | collective-permute-done | bytes 131104 | tf_op jit(solution)/shard_map/ppermute | solution.py:279
  45.5 1.8 %collective-permute-done.5 = bf16[128,512]{1,0:T(8,128)(2,1)S(1)} collective-permute-done((bf16[128,512]{1,0:T(8,128)(2,1)S(1)}, bf16[128,512]{1,0:T(8,128)(2,1)S(1)}, u32[]{:S(2)}, u32[]{:S(2)}) %collective-permute-start.5) | collective-permute-done | bytes 131104 | tf_op jit(solution)/shard_map/ppermute | solution.py:279
  47.4 0.1 add_convert_fusion
  47.4 0.7 %reshape.331 = bf16[32,2,2,512]{3,2,1,0:T(2,128)(2,1)} reshape(bf16[128,512]{1,0:T(8,128)(2,1)S(1)} %add_convert_fusion) | data formatting | bytes 262144 | tf_op jit(solution)/shard_map/reshape | solution.py:326
  (12 shorter events, 0.1 us)
Async XLA Ops:
  0.0 16.7 %copy-start = (f32[256]{0:T(256)S(1)}, f32[256]{0:T(256)}, u32[]{:S(2)}) copy-start(f32[256]{0:T(256)} %param.13) | copy-start | bytes 3076
  7.8 18.6 %all-to-all-start = ((bf16[16,16,512]{2,1,0:T(8,128)(2,1)}), bf16[16,16,512]{2,1,0:T(8,128)(2,1)S(1)}, u32[]{:S(2)}, u32[]{:S(2)}) async-start(bf16[16,16,512]{2,1,0:T(8,128)(2,1)} %bitcast.11), calls=%async_computation | async-start | bytes 524288 | tf_op jit(solution)/shard_map/all_to_all | solution.py:290
  17.7 0.7 %copy-start.3 = (f32[2]{0:T(128)S(1)}, f32[2]{0:T(128)}, u32[]{:S(2)}) copy-start(f32[2]{0:T(128)} %param.14) | copy-start | bytes 28
  18.4 0.7 %copy-start.2 = (s32[4]{0:T(128)S(1)}, s32[4]{0:T(128)}, u32[]{:S(2)}) copy-start(s32[4]{0:T(128)} %param.16) | copy-start | bytes 52
  19.0 0.7 %copy-start.1 = (f32[4]{0:T(128)S(1)}, f32[4]{0:T(128)}, u32[]{:S(2)}) copy-start(f32[4]{0:T(128)} %param.12) | copy-start | bytes 52
  26.6 6.4 %collective-permute-start.2 = (bf16[128,640]{1,0:T(8,128)(2,1)S(1)}, bf16[128,640]{1,0:T(8,128)(2,1)S(1)}, u32[]{:S(2)}, u32[]{:S(2)}) collective-permute-start(bf16[128,640]{1,0:T(8,128)(2,1)S(1)} %get-tuple-element.15), channel_id=1, source_target_pairs={{0,80},{1,241},{2,82},{3,243},{4,84},{5,245},{6,86},{7,247},{8,88}... | collective-permute-start | bytes 491528 | tf_op jit(solution)/shard_map/ppermute | solution.py:279
  28.5 6.1 %collective-permute-start = (bf16[128,640]{1,0:T(8,128)(2,1)S(1)}, bf16[128,640]{1,0:T(8,128)(2,1)S(1)}, u32[]{:S(2)}, u32[]{:S(2)}) collective-permute-start(bf16[128,640]{1,0:T(8,128)(2,1)S(1)} %get-tuple-element.16), channel_id=1, source_target_pairs={{0,16},{1,49},{2,18},{3,51},{4,20},{5,53},{6,22},{7,55},{8,24},{9,... | collective-permute-start | bytes 491528 | tf_op jit(solution)/shard_map/ppermute | solution.py:279
  28.9 5.8 %collective-permute-start.1 = (bf16[128,640]{1,0:T(8,128)(2,1)S(1)}, bf16[128,640]{1,0:T(8,128)(2,1)S(1)}, u32[]{:S(2)}, u32[]{:S(2)}) collective-permute-start(bf16[128,640]{1,0:T(8,128)(2,1)S(1)} %get-tuple-element.17), channel_id=1, source_target_pairs={{0,64},{1,193},{2,66},{3,195},{4,68},{5,197},{6,70},{7,199},{8,72}... | collective-permute-start | bytes 491528 | tf_op jit(solution)/shard_map/ppermute | solution.py:279
  35.6 8.4 %collective-permute-start.3 = (bf16[128,512]{1,0:T(8,128)(2,1)S(1)}, bf16[128,512]{1,0:T(8,128)(2,1)S(1)}, u32[]{:S(2)}, u32[]{:S(2)}) collective-permute-start(bf16[128,512]{1,0:T(8,128)(2,1)S(1)} %get-tuple-element.10), channel_id=1, source_target_pairs={{0,240},{1,81},{2,242},{3,83},{4,244},{5,85},{6,246},{7,87},{8,248... | collective-permute-start | bytes 393224 | tf_op jit(solution)/shard_map/ppermute | solution.py:279
  38.7 6.8 %collective-permute-start.4 = (bf16[128,512]{1,0:T(8,128)(2,1)S(1)}, bf16[128,512]{1,0:T(8,128)(2,1)S(1)}, u32[]{:S(2)}, u32[]{:S(2)}) collective-permute-start(bf16[128,512]{1,0:T(8,128)(2,1)S(1)} %get-tuple-element.11), channel_id=1, source_target_pairs={{0,192},{1,65},{2,194},{3,67},{4,196},{5,69},{6,198},{7,71},{8,200... | collective-permute-start | bytes 393224 | tf_op jit(solution)/shard_map/ppermute | solution.py:279
  41.2 6.2 %collective-permute-start.5 = (bf16[128,512]{1,0:T(8,128)(2,1)S(1)}, bf16[128,512]{1,0:T(8,128)(2,1)S(1)}, u32[]{:S(2)}, u32[]{:S(2)}) collective-permute-start(bf16[128,512]{1,0:T(8,128)(2,1)S(1)} %get-tuple-element.12), channel_id=1, source_target_pairs={{0,48},{1,17},{2,50},{3,19},{4,52},{5,21},{6,54},{7,23},{8,56},{9,... | collective-permute-start | bytes 393224 | tf_op jit(solution)/shard_map/ppermute | solution.py:279
